TPU v7x, 32 devices: a whole 2x2x4 slice. The times are simulated.
32 devices in a mesh: rows: 8 (over z, x), mp: 4 (over y, core).
Axes of the slice: x: 2, y: 2, z: 4, core: 2. Of those that a mesh axis runs over, the one named last changes fastest.
Arguments:
- hidden: bfloat16 [4096, 1536], P('rows'), may hold values from -6 to 6
- segments: int32 [8, 512], P('rows'), may hold values from 0 to 3, never falling along the last dimension, each value on 1 to 256 neighbouring positions
- granular: int32 [4096], P('rows'), may hold values from 0 to 3, as said below
- norm_gain: bfloat16 [2, 2, 1536], P(None, None, 'rows'), may hold values from 0.5 to 1.5
- norm_bias: bfloat16 [2, 2, 1536], P(None, None, 'rows'), may hold values from -1 to 1
- w_query: bfloat16 [2, 1536, 1536], P(None, 'rows', 'mp'), may hold values from -0.15625 to 0.15625
- w_key: bfloat16 [2, 1536, 1536], P(None, 'rows', 'mp'), may hold values from -0.15625 to 0.15625
- w_value: bfloat16 [2, 1536, 1536], P(None, 'rows', 'mp'), may hold values from -0.15625 to 0.15625
- w_out: bfloat16 [2, 1536, 1536], P(None, 'mp', 'rows'), may hold values from -0.625 to 0.625
- w_up: bfloat16 [2, 1536, 4, 1536], P(None, 'rows', 'mp'), may hold values from -0.15625 to 0.15625
- b_up: bfloat16 [2, 4, 1536], P(None, 'mp', 'rows'), may hold values from -3 to 3
- w_down: bfloat16 [2, 4, 1536, 1536], P(None, 'mp', None, 'rows'), may hold values from -0.15625 to 0.15625
- b_down: bfloat16 [2, 1536], P(None, 'rows'), may hold values from -2 to 2
- cotangent: bfloat16 [4096, 1536], P('rows'), may hold values from -6 to 6
Outputs:
- result: bfloat16 [4096, 1536], P('rows')
- grad_hidden: float32 [4096, 1536], P('rows')
- grad_norm_gain: float32 [2, 2, 1536], P(None, None, 'rows')
- grad_norm_bias: float32 [2, 2, 1536], P(None, None, 'rows')
- grad_query: float32 [2, 1536, 1536], P(None, 'rows', 'mp')
- grad_key: float32 [2, 1536, 1536], P(None, 'rows', 'mp')
- grad_value: float32 [2, 1536, 1536], P(None, 'rows', 'mp')
- grad_out: float32 [2, 1536, 1536], P(None, 'mp', 'rows')
- grad_up: float32 [2, 1536, 4, 1536], P(None, 'rows', 'mp')
- grad_up_bias: float32 [2, 4, 1536], P(None, 'mp', 'rows')
- grad_down: float32 [2, 4, 1536, 1536], P(None, 'mp', None, 'rows')
- grad_down_bias: float32 [2, 1536], P(None, 'rows')
Inputs may be any that keep to these rules, and one draw needn't show every extreme that they name: `granular`: in every block of 512 consecutive tokens (a device holds 4096 / rows tokens, so one or more such blocks), at most 256 have any one level; one level, drawn from the seed, has exactly 256 in every such block.
All inputs are finite; a program needn't handle non-finite values.
Results may differ from a plain program's by a relative error of at most 0.03.
Values may be sent and summed in bfloat16 or wider, within the bound.
No kernel may reach another device: no remote copies, remote signals or barrier semaphores. Data moves between devices by JAX's collectives and lax.ppermute only.
A program may use at most 320 MiB of HBM per device.

v0:
```python
from functools import partial

import jax
import jax.numpy as jnp
from jax import lax
from jax.sharding import PartitionSpec as P

DH = 128


epsilon = 1e-05
masked_value = -1e30


def as_sent(value):

    def short(part):
        return part.astype(jnp.bfloat16) if part.dtype == jnp.float32 else part

    return jax.tree.map(short, value)


def layer_norm(values, norm_scale, offset):
    average = jnp.mean(values, axis=-1, keepdims=True)
    centred = values - average
    variance = jnp.mean(centred * centred, axis=-1, keepdims=True)
    return centred * lax.rsqrt(variance + epsilon) * norm_scale + offset


def rotary_tables(length, head_width):
    half_width = head_width // 2
    frequency = 10000.0 ** (-jnp.arange(half_width, dtype=jnp.float32) / half_width)
    angles = jnp.arange(length, dtype=jnp.float32)[:, None] * frequency[None, :]
    return (jnp.cos(angles)[:, None, :], jnp.sin(angles)[:, None, :])


def rotate(values, cosine_table, sine_table):
    half_width = values.shape[-1] // 2
    leading = values[..., :half_width]
    trailing = values[..., half_width:]
    return jnp.concatenate(
        [
            leading * cosine_table - trailing * sine_table,
            trailing * cosine_table + leading * sine_table,
        ],
        axis=-1,
    )


def contract_rows(left, right):
    return lax.dot_general(
        left, right, (((0,), (0,)), ((), ())), preferred_element_type=jnp.float32
    )


def contract_cols(left, right):
    return lax.dot_general(
        left, right, (((1,), (1,)), ((), ())), preferred_element_type=jnp.float32
    )


def allowed_mask(segment_row):
    position = jnp.arange(segment_row.shape[0])
    return (position[:, None] >= position[None, :]) & (segment_row[:, None] == segment_row[None, :])


def score_block(query_block, key_block, segment_row):
    scale_factor = query_block.shape[-1] ** (-0.5)
    scores = (
        jnp.einsum("qhd,khd->hqk", query_block, key_block, preferred_element_type=jnp.float32)
        * scale_factor
    )
    return jnp.where(allowed_mask(segment_row)[None], scores, masked_value)


def attend_forward(inputs):
    query_block, key_block, value_block, segment_row = inputs
    scores = score_block(query_block, key_block, segment_row)
    highest = jnp.max(scores, axis=-1, keepdims=True)
    exponent = jnp.exp(scores - highest)
    totals = jnp.sum(exponent, axis=-1, keepdims=True)
    weights = (exponent / totals).astype(jnp.bfloat16)
    mixture = jnp.einsum("hqk,khd->qhd", weights, value_block, preferred_element_type=jnp.float32)
    return (mixture.astype(jnp.bfloat16), (highest + jnp.log(totals))[..., 0])


def attend_backward(inputs):
    query_block, key_block, value_block, segment_row, log_total, grad_mixture = inputs
    scale_factor = query_block.shape[-1] ** (-0.5)
    scores = score_block(query_block, key_block, segment_row)
    probs = jnp.exp(scores - log_total[..., None])
    grad_probs = jnp.einsum(
        "qhd,khd->hqk", grad_mixture, value_block, preferred_element_type=jnp.float32
    )
    inner = jnp.sum(probs * grad_probs, axis=-1, keepdims=True)
    grad_scores = (probs * (grad_probs - inner)).astype(jnp.bfloat16)
    grad_query = (
        jnp.einsum("hqk,khd->qhd", grad_scores, key_block, preferred_element_type=jnp.float32)
        * scale_factor
    )
    grad_key = (
        jnp.einsum("hqk,qhd->khd", grad_scores, query_block, preferred_element_type=jnp.float32)
        * scale_factor
    )
    grad_value = jnp.einsum(
        "hqk,qhd->khd", probs.astype(jnp.bfloat16), grad_mixture, preferred_element_type=jnp.float32
    )
    return (grad_query, grad_key, grad_value.astype(jnp.bfloat16))


def ffn_forward(prefix_level, received, up_weight, up_bias, down_weight):
    prefix_width = up_weight.shape[-1] // 8 * 2**prefix_level
    upward = jnp.dot(
        received, up_weight[:, 0, :prefix_width], preferred_element_type=jnp.float32
    ) + up_bias[0, :prefix_width].astype(jnp.float32)
    active = jax.nn.gelu(upward).astype(jnp.bfloat16)
    return jnp.dot(active, down_weight[0, :prefix_width, :], preferred_element_type=jnp.float32)


def ffn_backward(prefix_level, received, grad_out, up_weight, up_bias, down_weight):
    full_width = up_weight.shape[-1]
    prefix_width = full_width // 8 * 2**prefix_level
    up_matrix = up_weight[:, 0, :prefix_width]
    down_matrix = down_weight[0, :prefix_width, :]
    upward = jnp.dot(received, up_matrix, preferred_element_type=jnp.float32) + up_bias[
        0, :prefix_width
    ].astype(jnp.float32)
    active_full, gelu_pull = jax.vjp(jax.nn.gelu, upward)
    active = active_full.astype(jnp.bfloat16)
    grad_active = contract_cols(grad_out, down_matrix)
    grad_upward = gelu_pull(grad_active)[0].astype(jnp.bfloat16)
    grad_up_w = contract_rows(received, grad_upward)
    grad_up_b = jnp.sum(grad_upward.astype(jnp.float32), axis=0)
    grad_down_w = contract_rows(active, grad_out)
    grad_input = contract_cols(grad_upward, up_matrix)
    padding = full_width - prefix_width
    return (
        grad_input,
        jnp.pad(grad_up_w, ((0, 0), (0, padding))),
        jnp.pad(grad_up_b, (0, padding)),
        jnp.pad(grad_down_w, ((0, padding), (0, 0))),
    )


def shards(
    hidden,
    segments,
    granular,
    norm_gain,
    norm_bias,
    w_query,
    w_key,
    w_value,
    w_out,
    w_up,
    b_up,
    w_down,
    b_down,
    cotangent,
):
    rows_count = lax.axis_size("rows")
    layer_count = w_query.shape[0]
    tokens = hidden.shape[0]
    width = hidden.shape[1]
    seq_count, seq_length = segments.shape
    norm_gain, norm_bias, w_query, w_key, w_value, w_out, w_up, b_up, w_down, b_down = (
        lax.all_gather(norm_gain, "rows", axis=2, tiled=True),
        lax.all_gather(norm_bias, "rows", axis=2, tiled=True),
        lax.all_gather(w_query, "rows", axis=1, tiled=True),
        lax.all_gather(w_key, "rows", axis=1, tiled=True),
        lax.all_gather(w_value, "rows", axis=1, tiled=True),
        lax.all_gather(w_out, "rows", axis=2, tiled=True),
        lax.all_gather(w_up, "rows", axis=1, tiled=True),
        lax.all_gather(b_up, "rows", axis=2, tiled=True),
        lax.all_gather(w_down, "rows", axis=3, tiled=True),
        lax.all_gather(b_down, "rows", axis=1, tiled=True),
    )
    capacity = tokens // 2
    slot_rows = 4 * capacity // rows_count
    level_hot = (granular[:, None] == jnp.arange(4)[None, :]).astype(jnp.int32)
    earlier = jnp.cumsum(level_hot, axis=0) - level_hot
    standing = jnp.sum(earlier * level_hot, axis=1)
    slot_index = granular * capacity + standing
    dispatch = (jnp.arange(4 * capacity)[:, None] == slot_index[None, :]).astype(jnp.bfloat16)
    group_index = lax.axis_index("rows") // (rows_count // 4)
    cosine_table, sine_table = rotary_tables(seq_length, DH)
    forward_branches = [partial(ffn_forward, prefix_level) for prefix_level in range(4)]
    backward_branches = [partial(ffn_backward, prefix_level) for prefix_level in range(4)]

    def send_back(terms, bias_row):
        total = (
            jax.tree.map(lambda part: part.astype(jnp.float32), lax.psum(as_sent(terms), "mp"))
            + bias_row[None]
        ).astype(jnp.bfloat16)
        whole = lax.all_to_all(
            total.reshape(rows_count, slot_rows, width),
            "rows",
            split_axis=0,
            concat_axis=0,
            tiled=True,
        )
        return contract_rows(dispatch, whole.reshape(4 * capacity, width))

    activations = hidden.astype(jnp.float32)
    kept_values = []
    for layer_index in range(layer_count):
        gain_pair = norm_gain[layer_index].astype(jnp.float32)
        shifts = norm_bias[layer_index].astype(jnp.float32)
        normed = layer_norm(activations, gain_pair[0], shifts[0]).astype(jnp.bfloat16)
        query_rot = rotate(
            jnp.dot(normed, w_query[layer_index], preferred_element_type=jnp.float32).reshape(
                seq_count, seq_length, -1, DH
            ),
            cosine_table,
            sine_table,
        ).astype(jnp.bfloat16)
        key_rot = rotate(
            jnp.dot(normed, w_key[layer_index], preferred_element_type=jnp.float32).reshape(
                seq_count, seq_length, -1, DH
            ),
            cosine_table,
            sine_table,
        ).astype(jnp.bfloat16)
        value_low = (
            jnp.dot(normed, w_value[layer_index], preferred_element_type=jnp.float32)
            .reshape(seq_count, seq_length, -1, DH)
            .astype(jnp.bfloat16)
        )
        mixture, log_total = lax.map(attend_forward, (query_rot, key_rot, value_low, segments))
        mixture = mixture.reshape(tokens, -1)
        head_terms = jnp.dot(mixture, w_out[layer_index], preferred_element_type=jnp.float32)
        middle = activations + lax.psum(head_terms.astype(jnp.bfloat16), "mp").astype(jnp.float32)
        second = layer_norm(middle, gain_pair[1], shifts[1]).astype(jnp.bfloat16)
        outgoing = (
            jnp.dot(dispatch, second, preferred_element_type=jnp.float32)
            .astype(jnp.bfloat16)
            .reshape(rows_count, slot_rows, -1)
        )
        received = lax.all_to_all(
            outgoing, "rows", split_axis=0, concat_axis=0, tiled=True
        ).reshape(rows_count * slot_rows, -1)
        ffn_terms = lax.switch(
            group_index,
            forward_branches,
            received,
            w_up[layer_index],
            b_up[layer_index],
            w_down[layer_index],
        )
        combined = send_back(ffn_terms, b_down[layer_index].astype(jnp.float32))
        kept_values.append(
            (
                activations,
                normed,
                query_rot,
                key_rot,
                value_low,
                log_total,
                mixture,
                middle,
                received,
            )
        )
        activations = middle + combined
    result = activations.astype(jnp.bfloat16)
    grad_state = cotangent.astype(jnp.float32)
    zero_bias = jnp.zeros((width,), jnp.float32)
    layer_results = [None] * layer_count
    for layer_index in reversed(range(layer_count)):
        layer_input, normed, query_rot, key_rot, value_low, log_total, mixture, middle, received = (
            kept_values[layer_index]
        )
        gain_pair = norm_gain[layer_index].astype(jnp.float32)
        shifts = norm_bias[layer_index].astype(jnp.float32)
        grad_branch = grad_state.astype(jnp.bfloat16)
        grad_slots = (
            jnp.dot(dispatch, grad_branch, preferred_element_type=jnp.float32)
            .astype(jnp.bfloat16)
            .reshape(rows_count, slot_rows, -1)
        )
        grad_arrived = lax.all_to_all(
            grad_slots, "rows", split_axis=0, concat_axis=0, tiled=True
        ).reshape(rows_count * slot_rows, -1)
        grad_in_terms, grad_up_w, grad_up_b, grad_down_w = lax.switch(
            group_index,
            backward_branches,
            received,
            grad_arrived,
            w_up[layer_index],
            b_up[layer_index],
            w_down[layer_index],
        )
        grad_down_b = jnp.sum(grad_arrived.astype(jnp.float32), axis=0)
        grad_second = send_back(grad_in_terms, zero_bias)
        second_pull = jax.vjp(layer_norm, middle, gain_pair[1], shifts[1])[1]
        grad_mid_norm, grad_gain_two, grad_shift_two = second_pull(grad_second)
        grad_middle = grad_state + grad_mid_norm
        grad_attn = grad_middle.astype(jnp.bfloat16)
        grad_w_out = contract_rows(mixture, grad_attn)
        grad_mix = (
            contract_cols(grad_attn, w_out[layer_index])
            .astype(jnp.bfloat16)
            .reshape(seq_count, seq_length, -1, DH)
        )
        grad_q_rot, grad_k_rot, grad_v = lax.map(
            attend_backward, (query_rot, key_rot, value_low, segments, log_total, grad_mix)
        )
        grad_q = (
            rotate(grad_q_rot, cosine_table, -sine_table).reshape(tokens, -1).astype(jnp.bfloat16)
        )
        grad_k = (
            rotate(grad_k_rot, cosine_table, -sine_table).reshape(tokens, -1).astype(jnp.bfloat16)
        )
        grad_v = grad_v.reshape(tokens, -1)
        grad_w_query = contract_rows(normed, grad_q)
        grad_w_key = contract_rows(normed, grad_k)
        grad_w_value = contract_rows(normed, grad_v)
        grad_normed_terms = (
            contract_cols(grad_q, w_query[layer_index])
            + contract_cols(grad_k, w_key[layer_index])
            + contract_cols(grad_v, w_value[layer_index])
        )
        grad_normed = lax.psum(grad_normed_terms.astype(jnp.bfloat16), "mp").astype(jnp.float32)
        first_pull = jax.vjp(layer_norm, layer_input, gain_pair[0], shifts[0])[1]
        grad_in_state, grad_gain_one, grad_shift_one = first_pull(grad_normed)
        grad_state = grad_middle + grad_in_state
        layer_grads = (
            jnp.stack([grad_gain_one, grad_gain_two])[None],
            jnp.stack([grad_shift_one, grad_shift_two])[None],
            grad_w_query[None],
            grad_w_key[None],
            grad_w_value[None],
            grad_w_out[None],
            grad_up_w[:, None, :][None],
            grad_up_b[None][None],
            grad_down_w[None][None],
            grad_down_b[None],
        )
        layer_results[layer_index] = layer_grads
    stacked = tuple(
        (
            jnp.concatenate(
                [layer_results[layer_index][member] for layer_index in range(layer_count)], axis=0
            )
            for member in range(10)
        )
    )
    summed = (
        lax.psum_scatter(
            stacked[0].astype(jnp.bfloat16), "rows", scatter_dimension=2, tiled=True
        ).astype(jnp.float32),
        lax.psum_scatter(
            stacked[1].astype(jnp.bfloat16), "rows", scatter_dimension=2, tiled=True
        ).astype(jnp.float32),
        lax.psum_scatter(
            stacked[2].astype(jnp.bfloat16), "rows", scatter_dimension=1, tiled=True
        ).astype(jnp.float32),
        lax.psum_scatter(
            stacked[3].astype(jnp.bfloat16), "rows", scatter_dimension=1, tiled=True
        ).astype(jnp.float32),
        lax.psum_scatter(
            stacked[4].astype(jnp.bfloat16), "rows", scatter_dimension=1, tiled=True
        ).astype(jnp.float32),
        lax.psum_scatter(
            stacked[5].astype(jnp.bfloat16), "rows", scatter_dimension=2, tiled=True
        ).astype(jnp.float32),
        lax.psum_scatter(
            stacked[6].astype(jnp.bfloat16), "rows", scatter_dimension=1, tiled=True
        ).astype(jnp.float32),
        lax.psum_scatter(
            stacked[7].astype(jnp.bfloat16), "rows", scatter_dimension=2, tiled=True
        ).astype(jnp.float32),
        lax.psum_scatter(
            stacked[8].astype(jnp.bfloat16), "rows", scatter_dimension=3, tiled=True
        ).astype(jnp.float32),
        lax.psum_scatter(
            stacked[9].astype(jnp.bfloat16), "rows", scatter_dimension=1, tiled=True
        ).astype(jnp.float32),
    )
    return (
        result,
        grad_state,
        summed[0],
        summed[1],
        summed[2],
        summed[3],
        summed[4],
        summed[5],
        summed[6],
        summed[7],
        summed[8],
        summed[9],
    )


def solution(mesh):
    return jax.shard_map(
        shards,
        mesh=mesh,
        in_specs=(
            P("rows", None),
            P("rows", None),
            P("rows"),
            P(None, None, "rows"),
            P(None, None, "rows"),
            P(None, "rows", "mp"),
            P(None, "rows", "mp"),
            P(None, "rows", "mp"),
            P(None, "mp", "rows"),
            P(None, "rows", "mp", None),
            P(None, "mp", "rows"),
            P(None, "mp", None, "rows"),
            P(None, "rows"),
            P("rows", None),
        ),
        out_specs=(
            P("rows", None),
            P("rows", None),
            P(None, None, "rows"),
            P(None, None, "rows"),
            P(None, "rows", "mp"),
            P(None, "rows", "mp"),
            P(None, "rows", "mp"),
            P(None, "mp", "rows"),
            P(None, "rows", "mp", None),
            P(None, "mp", "rows"),
            P(None, "mp", None, "rows"),
            P(None, "rows"),
        ),
        check_vma=False,
    )
```

profile of v0, /device:TPU:0, one launch (start us, length us, event | category | flops | bytes accessed | tf_op | source)
XLA Modules:
  0.0 2731.9 jit_solution(16919373556068925884)
XLA Ops:
  14.5 35.0 %all_gather.31 = bf16[2,2,1536]{1,0,2:T(2,128)(2,1)S(1)} all-gather(bf16[2,2,192]{1,0,2:T(2,128)(2,1)S(1)} %copy.161), channel_id=1, replica_groups=mesh['rows'=8,'mp'=4] {'rows'}, dimensions={2}, use_global_device_ids=true | all-gather | bytes 13824 | tf_op jit(solution)/shard_map/all_gather | solution.py:168
  49.5 35.1 %all_gather.30 = bf16[2,2,1536]{1,0,2:T(2,128)(2,1)S(1)} all-gather(bf16[2,2,192]{1,0,2:T(2,128)(2,1)S(1)} %copy.160), channel_id=1, replica_groups=mesh['rows'=8,'mp'=4] {'rows'}, dimensions={2}, use_global_device_ids=true | all-gather | bytes 13824 | tf_op jit(solution)/shard_map/all_gather | solution.py:167
  86.4 25.1 slice_reduce_fusion.5
  113.4 25.3 slice_reduce_fusion.4
  150.3 37.1 %all-gather.10.cloned.1.call-done = bf16[2,1536,384]{2,1,0:T(8,128)(2,1)} async-done(((bf16[2,192,384]{2,1,0:T(8,128)(2,1)}), bf16[2,1536,384]{2,1,0:T(8,128)(2,1)}) %all-gather.10.cloned.1.call-update) | async-done | bytes 2359312 | tf_op jit(solution)/shard_map/all_gather | solution.py:169
  200.6 39.5 %all-gather.14.cloned.1.call-done = bf16[2,384,1536]{1,2,0:T(8,128)(2,1)} async-done(((bf16[2,384,192]{1,2,0:T(8,128)(2,1)}), bf16[2,384,1536]{1,2,0:T(8,128)(2,1)}) %all-gather.14.cloned.1.call-update) | async-done | bytes 2359312 | tf_op jit(solution)/shard_map/all_gather | solution.py:172
  248.4 36.7 %all-reduce.31.cloned.1.call-done = bf16[512,1536]{1,0:T(8,128)(2,1)} async-done(((bf16[512,1536]{1,0:T(8,128)(2,1)}), bf16[512,1536]{1,0:T(8,128)(2,1)}) %all-reduce.31.cloned.1.call-update) | async-done | bytes 1572880 | tf_op jit(solution)/shard_map/psum | solution.py:232
  292.3 5.6 all-to-all-start
  298.1 157.2 %all_gather.37 = bf16[2,1,1536]{1,0,2:T(2,128)(2,1)S(1)} all-gather(bf16[2,1,192]{1,0,2:T(2,128)(2,1)S(1)} %copy.169), channel_id=1, replica_groups=mesh['rows'=8,'mp'=4] {'rows'}, dimensions={2}, use_global_device_ids=true | all-gather | bytes 6912 | tf_op jit(solution)/shard_map/all_gather | solution.py:174
  455.3 12.5 slice_reduce_fusion.9
  467.8 23.4 all-gather.18.cloned.1.call-done
  491.2 19.1 fusion.554
  510.3 22.4 copy.244
  532.7 97.4 %all-gather.16.cloned.1.call-done = bf16[2,1536,1,1536]{3,1,2,0:T(8,128)(2,1)} async-done(((bf16[2,192,1,1536]{3,1,2,0:T(8,128)(2,1)}), bf16[2,1536,1,1536]{3,1,2,0:T(8,128)(2,1)}) %all-gather.16.cloned.1.call-update) | async-done | bytes 9437200 | tf_op jit(solution)/shard_map/all_gather | solution.py:173
  630.1 9.4 fusion.553
  639.5 20.1 conditional.4
  639.5 6.6 copy.172
  646.2 6.0 fusion.8
  660.3 18.9 all-gather
  679.9 47.8 %all-reduce.33.cloned.1.call-done = bf16[1024,1536]{1,0:T(8,128)(2,1)} async-done(((bf16[1024,1536]{1,0:T(8,128)(2,1)}), bf16[1024,1536]{1,0:T(8,128)(2,1)}) %all-reduce.33.cloned.1.call-update) | async-done | bytes 3145744 | tf_op jit(solution)/shard_map/psum | solution.py:192
  731.8 5.5 all-to-all-start.1
  737.3 26.5 slice_reduce_fusion.1
  763.8 26.6 slice_reduce_fusion
  801.2 6.8 all-to-all-done.1
  828.9 43.7 %all-reduce.35.cloned.1.call-done = bf16[512,1536]{1,0:T(8,128)(2,1)} async-done(((bf16[512,1536]{1,0:T(8,128)(2,1)}), bf16[512,1536]{1,0:T(8,128)(2,1)}) %all-reduce.35.cloned.1.call-update) | async-done | bytes 1572880 | tf_op jit(solution)/shard_map/psum | solution.py:232
  882.7 4.5 all-to-all-start.2
  887.2 22.4 copy.245
  909.7 47.6 %all-to-all-done.2 = bf16[8,128,1536]{2,1,0:T(8,128)(2,1)} async-done(((bf16[8,128,1536]{2,1,0:T(8,128)(2,1)}), bf16[8,128,1536]{2,1,0:T(8,128)(2,1)}, u32[]{:S(2)}, u32[]{:S(2)}) %all-to-all-start.2) | async-done | bytes 3145760 | tf_op jit(solution)/shard_map/all_to_all | solution.py:239
  957.3 71.5 %conditional.6 = (bf16[1024,1536]{1,0:T(8,128)(2,1)S(1)}, bf16[1,1,1536]{2,1,0:T(2,128)(2,1)S(1)}, bf16[1,1536,1,1536]{3,0,2,1:T(2,128)(2,1)}, bf16[1,1,1536,1536]{2,3,1,0:T(8,128)(2,1)}) conditional(s32[]{:T(128)} %clamp.2, (bf16[1,1536,1536]{2,1,0:T(8,128)(2,1)}, bf16[1024,1536]{1,0:T(8,128)(2,1)}, ...), branch_computations={%region_27.29_spmd, %region_29.31_spmd, %region_31.33_spmd, %regio... | conditional | flops 24214241280 | bytes 127439000 | solution.py:284
  957.3 6.6 copy.185
  983.2 6.6 copy.232
  989.8 23.0 copy.228
  1030.6 80.3 %all-reduce.37.cloned.1.call-done = bf16[8,128,1536]{2,1,0:T(8,128)(2,1)} async-done(((bf16[8,128,1536]{2,1,0:T(8,128)(2,1)}), bf16[8,128,1536]{2,1,0:T(8,128)(2,1)}) %all-reduce.37.cloned.1.call-update) | async-done | bytes 3145744 | tf_op jit(solution)/shard_map/psum | solution.py:192
  1110.8 5.5 all-to-all-start.5
  1116.4 70.6 %all-to-all-done.5 = bf16[8,128,1536]{2,1,0:T(8,128)(2,1)} async-done(((bf16[8,128,1536]{2,1,0:T(8,128)(2,1)}), bf16[8,128,1536]{2,1,0:T(8,128)(2,1)}, u32[]{:S(2)}, u32[]{:S(2)}) %all-to-all-start.5) | async-done | bytes 3145760 | tf_op jit(solution)/shard_map/all_to_all | solution.py:195
  1187.1 5.2 multiply_reduce_fusion
  1209.0 41.2 %all-reduce.39.cloned.1.call-done = bf16[512,1536]{1,0:T(8,128)(2,1)} async-done(((bf16[512,1536]{1,0:T(8,128)(2,1)}), bf16[512,1536]{1,0:T(8,128)(2,1)}) %all-reduce.39.cloned.1.call-update) | async-done | bytes 1572880 | tf_op jit(solution)/shard_map/psum | solution.py:323
  1258.2 76.0 %all_to_all.40 = bf16[8,128,1536]{2,1,0:T(8,128)(2,1)} all-to-all(bf16[8,128,1536]{2,1,0:T(8,128)(2,1)S(1)} %bitcast.567), channel_id=1, replica_groups=mesh['rows'=8,'mp'=4] {'rows'}, dimensions={0} | all-to-all | bytes 6291456 | tf_op jit(solution)/shard_map/all_to_all | solution.py:281
  1334.2 70.9 %conditional.7 = (bf16[1024,1536]{1,0:T(8,128)(2,1)S(1)}, bf16[1,1,1536]{2,1,0:T(2,128)(2,1)S(1)}, bf16[1,1536,1,1536]{3,0,2,1:T(2,128)(2,1)}, bf16[1,1,1536,1536]{2,3,1,0:T(8,128)(2,1)}) conditional(s32[]{:T(128)} %clamp.2, (bf16[1,1536,1536]{2,1,0:T(8,128)(2,1)}, bf16[1024,1536]{1,0:T(8,128)(2,1)}, ...), branch_computations={%region_42.44_spmd, %region_44.46_spmd, %region_46.48_spmd, %regio... | conditional | flops 24214241280 | bytes 127439000 | solution.py:284
  1334.2 6.7 copy.191
  1360.0 6.7 copy.240
  1366.7 23.1 copy.236
  1406.8 81.2 %all-reduce.41.cloned.1.call-done = bf16[8,128,1536]{2,1,0:T(8,128)(2,1)} async-done(((bf16[8,128,1536]{2,1,0:T(8,128)(2,1)}), bf16[8,128,1536]{2,1,0:T(8,128)(2,1)}) %all-reduce.41.cloned.1.call-update) | async-done | bytes 3145744 | tf_op jit(solution)/shard_map/psum | solution.py:192
  1487.9 5.5 all-to-all-start.7
  1493.6 20.9 conditional.5
  1493.6 6.8 copy.183
  1500.4 6.0 fusion.28
  1514.5 49.7 %all-to-all-done.7 = bf16[8,128,1536]{2,1,0:T(8,128)(2,1)} async-done(((bf16[8,128,1536]{2,1,0:T(8,128)(2,1)}), bf16[8,128,1536]{2,1,0:T(8,128)(2,1)}, u32[]{:S(2)}, u32[]{:S(2)}) %all-to-all-start.7) | async-done | bytes 3145760 | tf_op jit(solution)/shard_map/all_to_all | solution.py:195
  1564.2 5.4 multiply_reduce_fusion.1
  1607.3 71.4 %all-reduce.45.cloned.1.call-done = (bf16[1024,1536]{1,0:T(8,128)(2,1)}, bf16[512,1536]{1,0:T(8,128)(2,1)}) async-done(((bf16[1024,1536]{1,0:T(8,128)(2,1)}, bf16[512,1536]{1,0:T(8,128)(2,1)}), (bf16[1024,1536]{1,0:T(8,128)(2,1)}, bf16[512,1536]{1,0:T(8,128)(2,1)})) %all-reduce.45.cloned.1.call-update) | async-done | bytes 4718608 | tf_op jit(solution)/shard_map/psum | solution.py:192
  1709.7 22.3 pad_maximum_fusion
  1734.4 6.9 copy.197
  1741.4 8.3 pad_maximum_fusion.1
  1754.6 5.9 all-to-all-start.3
  1763.2 81.9 %reduce-scatter.29.cloned.1.call-done = bf16[192,2]{1,0:T(8,128)(2,1)} async-done(((bf16[1536,2]{1,0:T(8,128)(2,1)}), bf16[192,2]{1,0:T(8,128)(2,1)}) %reduce-scatter.29.cloned.1.call-update) | async-done | bytes 784
  1846.9 4.6 add_add_fusion.4
  1851.6 57.7 %reduce-scatter.25.cloned.1.call-done = bf16[192,4]{1,0:T(8,128)(2,1)} async-done(((bf16[1536,4]{1,0:T(8,128)(2,1)}), bf16[192,4]{1,0:T(8,128)(2,1)}) %reduce-scatter.25.cloned.1.call-update) | async-done | bytes 1552
  1910.9 62.5 %reduce-scatter.27.cloned.1.call-done = bf16[192,4]{1,0:T(8,128)(2,1)} async-done(((bf16[1536,4]{1,0:T(8,128)(2,1)}), bf16[192,4]{1,0:T(8,128)(2,1)}) %reduce-scatter.27.cloned.1.call-update) | async-done | bytes 1552
  1975.0 69.8 %reduce-scatter.21.cloned.1.call-done = bf16[2,192,384]{2,1,0:T(8,128)(2,1)} async-done(((bf16[2,1536,384]{2,1,0:T(8,128)(2,1)}), bf16[2,192,384]{2,1,0:T(8,128)(2,1)}) %reduce-scatter.21.cloned.1.call-update) | async-done | bytes 294928 | tf_op jit(solution)/shard_map/reduce_scatter | solution.py:361
  2046.6 70.3 %reduce-scatter.17.cloned.1.call-done = bf16[2,192,384]{2,1,0:T(8,128)(2,1)} async-done(((bf16[2,1536,384]{2,1,0:T(8,128)(2,1)}), bf16[2,192,384]{2,1,0:T(8,128)(2,1)}) %reduce-scatter.17.cloned.1.call-update) | async-done | bytes 294928 | tf_op jit(solution)/shard_map/reduce_scatter | solution.py:355
  2118.7 70.2 %reduce-scatter.19.cloned.1.call-done = bf16[2,192,384]{2,1,0:T(8,128)(2,1)} async-done(((bf16[2,1536,384]{2,1,0:T(8,128)(2,1)}), bf16[2,192,384]{2,1,0:T(8,128)(2,1)}) %reduce-scatter.19.cloned.1.call-update) | async-done | bytes 294928 | tf_op jit(solution)/shard_map/reduce_scatter | solution.py:358
  2190.7 4.9 fusion.417
  2195.5 359.6 %all-reduce.43.cloned.1.call-done = (bf16[2,384,1536]{1,0,2:T(2,128)(2,1)}, bf16[2,1536,1,1536]{3,0,2,1:T(2,128)(2,1)}) async-done(((bf16[2,384,1536]{1,0,2:T(2,128)(2,1)}, bf16[2,1536,1,1536]{3,0,2,1:T(2,128)(2,1)}), (bf16[2,384,1536]{1,0,2:T(2,128)(2,1)}, bf16[2,1536,1,1536]{3,0,2,1:T(2,128)(2,1)})) %all-reduce.43.cloned.1.call-update) | async-done | bytes 11796496
  2563.1 158.5 %reduce-scatter.23.cloned.1.call-done = bf16[2,1,1536,192]{2,3,1,0:T(8,128)(2,1)} async-done(((bf16[2,1,1536,1536]{2,3,1,0:T(8,128)(2,1)}), bf16[2,1,1536,192]{2,3,1,0:T(8,128)(2,1)}) %reduce-scatter.23.cloned.1.call-update) | async-done | bytes 1179664 | tf_op jit(solution)/shard_map/reduce_scatter | solution.py:373
  (556 shorter events, 262.7 us)
Async XLA Ops:
  7.2 134.2 %all-gather.8.cloned.1.call-start = ((), (), s32[]{:S(2)}) async-start(), calls=%async_computation.16 | async-start | bytes 2654208 | tf_op jit(solution)/shard_map/all_gather | solution.py:171
  7.9 137.9 %all-gather.12.cloned.1.call-start = ((), (), s32[]{:S(2)}) async-start(), calls=%async_computation.18 | async-start | bytes 2654208 | tf_op jit(solution)/shard_map/all_gather | solution.py:170
  8.7 178.7 %all-gather.10.cloned.1.call-start = ((), (), s32[]{:S(2)}) async-start(), calls=%async_computation.17 | async-start | bytes 2654208 | tf_op jit(solution)/shard_map/all_gather | solution.py:169
  9.4 230.7 %all-gather.14.cloned.1.call-start = ((), (), s32[]{:S(2)}) async-start(), calls=%async_computation.19 | async-start | bytes 2654208 | tf_op jit(solution)/shard_map/all_gather | solution.py:172
  10.0 275.1 %all-reduce.31.cloned.1.call-start = ((), (), s32[]{:S(2)}) async-start(), calls=%async_computation.20 | async-start | bytes 3145728 | tf_op jit(solution)/shard_map/psum | solution.py:232
  11.8 126.9 %copy-start.94 = (f32[512]{0:T(512)}, f32[512]{0:T(512)S(1)}, u32[]{:S(2)}) copy-start(f32[512]{0:T(512)S(1)} %broadcast_multiply_fusion.3) | copy-start | bytes 6148
  12.9 125.8 %copy-start.106 = (f32[512]{0:T(512)}, f32[512]{0:T(512)S(1)}, u32[]{:S(2)}) copy-start(f32[512]{0:T(512)S(1)} %fusion.537) | copy-start | bytes 6148
  14.5 807.4 %copy-start.36 = (f32[512,64]{0,1:T(8,128)}, f32[512,64]{0,1:T(8,128)S(1)}, u32[]{:S(2)}) copy-start(f32[512,64]{0,1:T(8,128)S(1)} %get-tuple-element.692) | copy-start | bytes 393220
  111.5 176.9 %copy-start.102 = (f32[1536]{0:T(1024)}, f32[1536]{0:T(1024)S(1)}, u32[]{:S(2)}) copy-start(f32[1536]{0:T(1024)S(1)} %get-tuple-element.616) | copy-start | bytes 18436
  243.6 247.7 %all-gather.18.cloned.1.call-start = ((), (), s32[]{:S(2)}) async-start(), calls=%async_computation.22 | async-start | bytes 10616832 | tf_op jit(solution)/shard_map/all_gather | solution.py:175
  245.9 384.2 %all-gather.16.cloned.1.call-start = ((), (), s32[]{:S(2)}) async-start(), calls=%async_computation.21 | async-start | bytes 10616832 | tf_op jit(solution)/shard_map/all_gather | solution.py:173
  248.4 627.4 %copy-start.148 = (s32[512]{0:T(512)}, s32[512]{0:T(512)S(1)}, u32[]{:S(2)}) copy-start(s32[512]{0:T(512)S(1)} %multiply_add_fusion.7) | copy-start | bytes 6148
  292.3 347.2 %all-to-all-start = ((bf16[8,128,1536]{2,1,0:T(8,128)(2,1)}), bf16[8,128,1536]{2,1,0:T(8,128)(2,1)}, u32[]{:S(2)}, u32[]{:S(2)}) async-start(bf16[8,128,1536]{2,1,0:T(8,128)(2,1)} %bitcast.565), calls=%async_computation | async-start | bytes 6291456 | tf_op jit(solution)/shard_map/all_to_all | solution.py:239
  297.9 429.8 %all-reduce.33.cloned.1.call-start = ((), (), s32[]{:S(2)}) async-start(), calls=%async_computation.23 | async-start | bytes 6291456 | tf_op jit(solution)/shard_map/psum | solution.py:192
  467.8 171.7 %copy-start.98 = (bf16[1,1536]{1,0:T(2,128)(2,1)}, bf16[1,1536]{1,0:T(2,128)(2,1)S(1)}, u32[]{:S(2)}) copy-start(bf16[1,1536]{1,0:T(2,128)(2,1)S(1)} %squeeze.204) | copy-start | bytes 9220
  731.8 76.2 %all-to-all-start.1 = ((bf16[8,128,1536]{2,1,0:T(8,128)(2,1)}), bf16[8,128,1536]{2,1,0:T(8,128)(2,1)}, u32[]{:S(2)}, u32[]{:S(2)}) async-start(bf16[8,128,1536]{2,1,0:T(8,128)(2,1)} %bitcast.542), calls=%async_computation.1 | async-start | bytes 6291456 | tf_op jit(solution)/shard_map/all_to_all | solution.py:195
  737.3 53.2 %copy-start.31 = (bf16[512,1536]{1,0:T(8,128)(2,1)S(1)}, bf16[512,1536]{1,0:T(8,128)(2,1)}, u32[]{:S(2)}) copy-start(bf16[512,1536]{1,0:T(8,128)(2,1)} %param.43) | copy-start | bytes 4718596
  763.8 54.7 %copy-start.92 = (f32[1536]{0:T(1024)}, f32[1536]{0:T(1024)S(1)}, u32[]{:S(2)}) copy-start(f32[1536]{0:T(1024)S(1)} %get-tuple-element.613) | copy-start | bytes 18436
  763.8 112.0 %copy-start.104 = (f32[1536]{0:T(1024)}, f32[1536]{0:T(1024)S(1)}, u32[]{:S(2)}) copy-start(f32[1536]{0:T(1024)S(1)} %get-tuple-element.612) | copy-start | bytes 18436
  808.0 74.6 %all-to-all-start.4 = ((bf16[8,128,1536]{2,1,0:T(8,128)(2,1)}), bf16[8,128,1536]{2,1,0:T(8,128)(2,1)}, u32[]{:S(2)}, u32[]{:S(2)}) async-start(bf16[8,128,1536]{2,1,0:T(8,128)(2,1)} %bitcast.566), calls=%async_computation.4 | async-start | bytes 6291456 | tf_op jit(solution)/shard_map/all_to_all | solution.py:281
  812.5 60.1 %all-reduce.35.cloned.1.call-start = ((), (), s32[]{:S(2)}) async-start(), calls=%async_computation.24 | async-start | bytes 3145728 | tf_op jit(solution)/shard_map/psum | solution.py:232
  882.7 74.6 %all-to-all-start.2 = ((bf16[8,128,1536]{2,1,0:T(8,128)(2,1)}), bf16[8,128,1536]{2,1,0:T(8,128)(2,1)}, u32[]{:S(2)}, u32[]{:S(2)}) async-start(bf16[8,128,1536]{2,1,0:T(8,128)(2,1)} %bitcast.111), calls=%async_computation.2 | async-start | bytes 6291456 | tf_op jit(solution)/shard_map/all_to_all | solution.py:239
  887.1 223.7 %all-reduce.37.cloned.1.call-start = ((), (), s32[]{:S(2)}) async-start(), calls=%async_computation.25 | async-start | bytes 6291456 | tf_op jit(solution)/shard_map/psum | solution.py:192
  887.2 70.1 %copy-start.100 = (bf16[1,1536]{1,0:T(2,128)(2,1)}, bf16[1,1536]{1,0:T(2,128)(2,1)S(1)}, u32[]{:S(2)}) copy-start(bf16[1,1536]{1,0:T(2,128)(2,1)S(1)} %squeeze.211) | copy-start | bytes 9220
  1030.5 85.9 %copy-start.114 = (f32[3,512]{1,0:T(4,128)S(1)}, f32[3,512]{1,0:T(4,128)}, u32[]{:S(2)}) copy-start(f32[3,512]{1,0:T(4,128)} %copy-done.113) | copy-start | bytes 18436
  1030.5 85.9 %copy-start.116 = (f32[3,512]{1,0:T(4,128)S(1)}, f32[3,512]{1,0:T(4,128)}, u32[]{:S(2)}) copy-start(f32[3,512]{1,0:T(4,128)} %copy-done.115) | copy-start | bytes 18436
  1030.5 156.5 %copy-start.12 = (f32[512,1536]{1,0:T(8,128)S(1)}, f32[512,1536]{1,0:T(8,128)}, u32[]{:S(2)}) copy-start(f32[512,1536]{1,0:T(8,128)} %copy-done.11) | copy-start | bytes 9437188
  1030.5 156.5 %copy-start.105 = (f32[1536]{0:T(1024)S(1)}, f32[1536]{0:T(1024)}, u32[]{:S(2)}) copy-start(f32[1536]{0:T(1024)} %copy-done.104) | copy-start | bytes 18436
  1030.5 156.5 %copy-start.128 = (f32[512]{0:T(512)S(1)}, f32[512]{0:T(512)}, u32[]{:S(2)}) copy-start(f32[512]{0:T(512)} %copy-done.127) | copy-start | bytes 6148
  1030.5 156.5 %copy-start.142 = (f32[512]{0:T(512)S(1)}, f32[512]{0:T(512)}, u32[]{:S(2)}) copy-start(f32[512]{0:T(512)} %copy-done.141) | copy-start | bytes 6148
  1030.6 156.5 %copy-start.149 = (s32[512]{0:T(512)S(1)}, s32[512]{0:T(512)}, u32[]{:S(2)}) copy-start(s32[512]{0:T(512)} %copy-done.148) | copy-start | bytes 6148
  1110.8 76.2 %all-to-all-start.5 = ((bf16[8,128,1536]{2,1,0:T(8,128)(2,1)}), bf16[8,128,1536]{2,1,0:T(8,128)(2,1)}, u32[]{:S(2)}, u32[]{:S(2)}) async-start(bf16[8,128,1536]{2,1,0:T(8,128)(2,1)} %all-reduce.37.cloned.1.call-done), calls=%async_computation.5 | async-start | bytes 6291456 | tf_op jit(solution)/shard_map/all_to_all | solution.py:195
  1116.3 133.9 %all-reduce.39.cloned.1.call-start = ((), (), s32[]{:S(2)}) async-start(), calls=%async_computation.26 | async-start | bytes 3145728 | tf_op jit(solution)/shard_map/psum | solution.py:323
  1208.8 279.1 %all-reduce.41.cloned.1.call-start = ((), (), s32[]{:S(2)}) async-start(), calls=%async_computation.27 | async-start | bytes 6291456 | tf_op jit(solution)/shard_map/psum | solution.py:192
  1258.2 76.0 %copy-start.99 = (bf16[1,1536]{1,0:T(2,128)(2,1)S(1)}, bf16[1,1536]{1,0:T(2,128)(2,1)}, u32[]{:S(2)}) copy-start(bf16[1,1536]{1,0:T(2,128)(2,1)} %copy-done.98) | copy-start | bytes 9220
  1406.7 86.7 %copy-start.110 = (f32[3,512]{1,0:T(4,128)S(1)}, f32[3,512]{1,0:T(4,128)}, u32[]{:S(2)}) copy-start(f32[3,512]{1,0:T(4,128)} %copy-done.109) | copy-start | bytes 18436
  1406.7 86.7 %copy-start.112 = (f32[3,512]{1,0:T(4,128)S(1)}, f32[3,512]{1,0:T(4,128)}, u32[]{:S(2)}) copy-start(f32[3,512]{1,0:T(4,128)} %copy-done.111) | copy-start | bytes 18436
  1406.8 86.8 %copy-start.101 = (bf16[1,1536]{1,0:T(2,128)(2,1)S(1)}, bf16[1,1536]{1,0:T(2,128)(2,1)}, u32[]{:S(2)}) copy-start(bf16[1,1536]{1,0:T(2,128)(2,1)} %copy-done.100) | copy-start | bytes 9220
  1487.9 76.2 %all-to-all-start.7 = ((bf16[8,128,1536]{2,1,0:T(8,128)(2,1)}), bf16[8,128,1536]{2,1,0:T(8,128)(2,1)}, u32[]{:S(2)}, u32[]{:S(2)}) async-start(bf16[8,128,1536]{2,1,0:T(8,128)(2,1)} %all-reduce.41.cloned.1.call-done), calls=%async_computation.7 | async-start | bytes 6291456 | tf_op jit(solution)/shard_map/all_to_all | solution.py:195
  1493.4 185.3 %all-reduce.45.cloned.1.call-start = ((), (), s32[]{:S(2)}) async-start(), calls=%async_computation.37 | async-start | bytes 9437184 | tf_op jit(solution)/shard_map/psum | solution.py:192
  1493.5 70.6 %copy-start.1 = (bf16[512,1536]{1,0:T(8,128)(2,1)S(1)}, bf16[512,1536]{1,0:T(8,128)(2,1)}, u32[]{:S(2)}) copy-start(bf16[512,1536]{1,0:T(8,128)(2,1)} %param.30) | copy-start | bytes 4718596
  1493.5 70.6 %copy-start.22 = (bf16[512,1536]{1,0:T(8,128)(2,1)S(1)}, bf16[512,1536]{1,0:T(8,128)(2,1)}, u32[]{:S(2)}) copy-start(bf16[512,1536]{1,0:T(8,128)(2,1)} %all-reduce.31.cloned.1.call-done) | copy-start | bytes 4718596
  1493.5 70.6 %copy-start.103 = (f32[1536]{0:T(1024)S(1)}, f32[1536]{0:T(1024)}, u32[]{:S(2)}) copy-start(f32[1536]{0:T(1024)} %copy-done.102) | copy-start | bytes 18436
  1493.6 70.6 %copy-start.126 = (f32[512]{0:T(512)S(1)}, f32[512]{0:T(512)}, u32[]{:S(2)}) copy-start(f32[512]{0:T(512)} %copy-done.125) | copy-start | bytes 6148
  1493.6 70.6 %copy-start.140 = (f32[512]{0:T(512)S(1)}, f32[512]{0:T(512)}, u32[]{:S(2)}) copy-start(f32[512]{0:T(512)} %copy-done.139) | copy-start | bytes 6148
  1493.6 70.6 %copy-start.150 = (s32[512]{0:T(512)S(1)}, s32[512]{0:T(512)}, u32[]{:S(2)}) copy-start(s32[512]{0:T(512)} %copy-done.148) | copy-start | bytes 6148
  1585.9 175.8 %reduce-scatter.31.cloned.1.call-start = ((), (), s32[]{:S(2)}) async-start(), calls=%async_computation.35 | async-start | bytes 442368
  1599.4 79.3 %copy-start.91 = (f32[1536]{0:T(1024)S(1)}, f32[1536]{0:T(1024)}, u32[]{:S(2)}) copy-start(f32[1536]{0:T(1024)} %copy-done.90) | copy-start | bytes 18436
  1599.4 79.3 %copy-start.95 = (f32[512]{0:T(512)S(1)}, f32[512]{0:T(512)}, u32[]{:S(2)}) copy-start(f32[512]{0:T(512)} %copy-done.94) | copy-start | bytes 6148
  1600.2 244.9 %reduce-scatter.29.cloned.1.call-start = ((), (), s32[]{:S(2)}) async-start(), calls=%async_computation.34 | async-start | bytes 442368
  1603.7 305.6 %reduce-scatter.25.cloned.1.call-start = ((), (), s32[]{:S(2)}) async-start(), calls=%async_computation.32 | async-start | bytes 442368
  1607.3 74.0 %copy-start.130 = (f32[512]{0:T(512)S(1)}, f32[512]{0:T(512)}, u32[]{:S(2)}) copy-start(f32[512]{0:T(512)} %copy-done.129) | copy-start | bytes 6148
  1607.3 74.0 %copy-start.107 = (f32[512]{0:T(512)S(1)}, f32[512]{0:T(512)}, u32[]{:S(2)}) copy-start(f32[512]{0:T(512)} %copy-done.106) | copy-start | bytes 6148
  1688.1 285.2 %reduce-scatter.27.cloned.1.call-start = ((), (), s32[]{:S(2)}) async-start(), calls=%async_computation.33 | async-start | bytes 442368
  1692.9 351.9 %reduce-scatter.21.cloned.1.call-start = ((), (), s32[]{:S(2)}) async-start(), calls=%async_computation.30 | async-start | bytes 2654208 | tf_op jit(solution)/shard_map/reduce_scatter | solution.py:361
  1696.4 420.5 %reduce-scatter.17.cloned.1.call-start = ((), (), s32[]{:S(2)}) async-start(), calls=%async_computation.28 | async-start | bytes 2654208 | tf_op jit(solution)/shard_map/reduce_scatter | solution.py:355
  1702.0 486.8 %reduce-scatter.19.cloned.1.call-start = ((), (), s32[]{:S(2)}) async-start(), calls=%async_computation.29 | async-start | bytes 2654208 | tf_op jit(solution)/shard_map/reduce_scatter | solution.py:358
  1707.4 847.8 %all-reduce.43.cloned.1.call-start = ((), (), s32[]{:S(2)}) async-start(), calls=%async_computation.36 | async-start | bytes 23592960
  1741.3 980.3 %reduce-scatter.23.cloned.1.call-start = ((), (), s32[]{:S(2)}) async-start(), calls=%async_computation.31 | async-start | bytes 10616832 | tf_op jit(solution)/shard_map/reduce_scatter | solution.py:373
  1754.6 92.4 %copy-start.143 = (f32[512]{0:T(512)S(1)}, f32[512]{0:T(512)}, u32[]{:S(2)}) copy-start(f32[512]{0:T(512)} %get-tuple-element.607) | copy-start | bytes 6148
  1754.6 92.4 %copy-start.124 = (f32[512]{0:T(512)S(1)}, f32[512]{0:T(512)}, u32[]{:S(2)}) copy-start(f32[512]{0:T(512)} %copy-done.123) | copy-start | bytes 6148
  1754.6 436.1 %all-to-all-start.3 = ((bf16[8,128,1536]{2,1,0:T(8,128)(2,1)}), bf16[8,128,1536]{2,1,0:T(8,128)(2,1)}, u32[]{:S(2)}, u32[]{:S(2)}) async-start(bf16[8,128,1536]{2,1,0:T(8,128)(2,1)} %bitcast.541), calls=%async_computation.3 | async-start | bytes 6291456 | tf_op jit(solution)/shard_map/all_to_all | solution.py:195
  1851.6 339.1 %copy-start.13 = (f32[512,1536]{1,0:T(8,128)S(1)}, f32[512,1536]{1,0:T(8,128)}, u32[]{:S(2)}) copy-start(f32[512,1536]{1,0:T(8,128)} %copy-done.11) | copy-start | bytes 9437188
  1851.6 339.1 %copy-start.151 = (s32[512]{0:T(512)S(1)}, s32[512]{0:T(512)}, u32[]{:S(2)}) copy-start(s32[512]{0:T(512)} %copy-done.148) | copy-start | bytes 6148
  (120 other events, 728.5 us)
Sparse Core Ops, SparseCore 0:
  10.2 68.7 all-gather.7
  81.2 53.2 all-gather.11
  136.7 50.6 all-gather.9
  189.4 50.6 all-gather.13
  243.7 41.3 all-reduce.30
  287.1 204.0 all-gather.17
  493.4 136.6 all-gather.15
  659.8 67.8 all-reduce.32
  829.0 43.5 all-reduce.34
  1030.6 80.1 all-reduce.36
  1208.9 41.2 all-reduce.38
  1406.9 81.0 all-reduce.40
  1586.0 92.6 all-reduce.44
  1681.8 61.5 reduce-scatter.30
  1746.5 98.6 reduce-scatter.28
  1848.8 60.3 reduce-scatter.24
  1913.0 60.3 reduce-scatter.26
  1976.7 67.9 reduce-scatter.20
  2048.8 67.9 reduce-scatter.16
  2120.8 68.0 reduce-scatter.18
  2193.0 362.1 all-reduce.42
  2559.2 162.3 reduce-scatter.22
where the time goes:
time: 2750 us; the launch traced here: 2730 us
  waiting for transfers between devices  1710 us (62%)
  local copies, waits for them, and re-layouts  367 us (13%)
  blocking collectives  322 us (12%)
  matrix products  120 us (4%)
  other arithmetic  107 us (4%)
  loops' own time  47 us (2%)
  starting transfers between devices  38.9 us (1%)
    unnamed x27, waiting for transfers between devices  565 us
    psum x4, waiting for transfers between devices, send_back(): lax.psum(as_sent(terms), 'mp')  281 us
    reduce_scatter x1, waiting for transfers between devices, shards(): lax.psum_scatter(stacked[8].astype(jnp.bfloat16), 'rows', scatter_dimensi...  159 us
    all_gather x1, blocking collectives, shards(): lax.all_gather(b_up, 'rows', axis=2, tiled=True)  157 us
    all_to_all x4, waiting for transfers between devices, send_back(): lax.all_to_all(total.reshape(rows_count, slot_rows, width), 'rows', split...  127 us
    slice x4, local copies, waits for them, and re-layouts, shards(): second = layer_norm(middle, gain_pair[1], shifts[1]).astype(jnp.bfloat16)  104 us
    all_gather x1, waiting for transfers between devices, shards(): lax.all_gather(w_up, 'rows', axis=1, tiled=True)  97.4 us
    unnamed x334, local copies, waits for them, and re-layouts  96.1 us
  transfers between devices with their start and end apart: 29, of which 24 were waited for; matrix products, arithmetic and copies ran while one was open for 15% of the time, Pallas kernels for 0%

commit v1 on v0

v1 whole, which is shorter than its diff:
```python
from functools import partial

import jax
import jax.numpy as jnp
from jax import lax
from jax.experimental import pallas as pl
from jax.experimental.pallas import tpu as pltpu
from jax.sharding import PartitionSpec as P

DH = 128

epsilon = 1e-05
masked_value = -1e30
bf16 = jnp.bfloat16
f32 = jnp.float32


def ring_order(count):
    return list(range(0, count, 2)) + list(range(count - 1, 0, -2))


def whole_blocks(pieces):
    middle = len(pieces) // 2
    return [
        *pieces[:middle],
        jnp.concatenate(pieces[middle : middle + 2], axis=1),
        *pieces[middle + 2 :],
    ]


def tie(*values):
    return lax.optimization_barrier(values)


class Ring:
    def __init__(self, count):
        self.count = count
        self.middle = count // 2
        order = ring_order(count)
        places = [0] * count
        for place, device in enumerate(order):
            places[device] = place
        place = jnp.asarray(places, jnp.int32)[lax.axis_index("rows")]
        self.owners = jnp.asarray(order, jnp.int32)[(place + jnp.arange(count)) % count]
        self.pairs = [(order[i], order[(i + 1) % count]) for i in range(count)]

    def ahead(self, value):
        return lax.ppermute(value, "rows", self.pairs)

    def back(self, value):
        return lax.ppermute(value, "rows", [(b, a) for a, b in self.pairs])


def half_of(extent):
    half = extent // 2
    whole_tiles = (half + 15) // 16 * 16
    return whole_tiles if whole_tiles < extent else half


class Gather:
    handling = 2.2

    def __init__(self, ring, shard):
        self.ring, self.shard = ring, shard
        self.extent = shard.shape[1]
        self.step, self.head, self.tail = 0, [shard], []

    @property
    def done(self):
        return self.step == self.ring.middle

    @property
    def pieces(self):
        return self.head + self.tail

    def start(self, value):
        if self.step == 0:
            value, self.shard = tie(value, self.shard)
            self.head = [self.shard]
            self.forward = self.backward = self.shard
        self.step += 1
        if self.step == self.ring.middle:
            half = half_of(self.extent)
            value, self.forward, self.backward = tie(
                value, self.forward[:, :half], self.backward[:, half:]
            )
        self.size = self.forward.size * 2
        self.flight = self.ring.ahead(self.forward), self.ring.back(self.backward)
        return value

    def finish(self, value):
        value, self.forward, self.backward = tie(value, *self.flight)
        if self.step < self.ring.middle:
            self.head.append(self.backward)
            self.tail.insert(0, self.forward)
        else:
            self.tail = [self.forward, self.backward] + self.tail
        return value


class Scatter:
    handling = 4.5

    def __init__(self, ring, *terms):
        self.ring, self.terms = ring, terms
        self.extent = terms[0].shape[0] // ring.count
        self.step, self.total = 0, None

    @property
    def done(self):
        return self.step == self.ring.middle

    def block(self, place, first=0, last=None):
        last = self.extent if last is None else last
        start = place * self.extent
        return jnp.stack([part[start + first : start + last].astype(f32) for part in self.terms])

    def start(self, value):
        half, count, middle = half_of(self.extent), self.ring.count, self.ring.middle
        if self.step == 0:
            forward = self.block(middle, 0, half)
            backward = self.block(middle, half)
        else:
            forward = self.block(middle - self.step)
            backward = self.block(count - middle + self.step)
            if self.step == 1:
                forward = jnp.concatenate(
                    [forward[:, :half] + self.forward, forward[:, half:]], axis=1
                )
                backward = jnp.concatenate(
                    [backward[:, :half], backward[:, half:] + self.backward], axis=1
                )
            else:
                forward = forward + self.forward
                backward = backward + self.backward
        value, forward, backward = tie(value, forward.astype(bf16), backward.astype(bf16))
        self.step += 1
        self.size = forward.size * 2
        self.flight = self.ring.ahead(forward), self.ring.back(backward)
        return value

    def finish(self, value):
        value, forward, backward = tie(value, *self.flight)
        self.forward, self.backward = forward.astype(f32), backward.astype(f32)
        if self.done:
            self.total = self.block(0) + self.forward + self.backward
        return value


class Belt:
    rate = 0.0214
    lag = 2.0
    patience = 4.0

    def __init__(self, depth):
        self.depth, self.waiting, self.flying = depth, [], []
        self.clock = self.free = 0.0
        self.tight = False

    def add(self, *chains):
        self.waiting.extend(chains)

    def launch(self, value):
        while self.waiting and len(self.flying) < self.depth:
            chain = self.waiting.pop(0)
            value = chain.start(value)
            self.clock += chain.handling
            self.free = max(self.clock, self.free) + chain.size / 1e3 * self.rate
            self.flying.append((self.free + self.lag, chain))
        return value

    def end_first(self, value):
        finish, chain = self.flying.pop(0)
        self.clock = max(self.clock, finish)
        value = chain.finish(value)
        if not chain.done:
            self.waiting.insert(sum(other.step > 0 for other in self.waiting), chain)
        return self.launch(value)

    def catch_up(self, value, until):
        while self.flying and self.flying[0][0] <= until:
            value = self.end_first(value)
        return self.launch(value)

    def busy(self, value, time):
        self.clock += time
        return self.catch_up(value, self.clock + self.patience)

    def idle(self, value, time):
        if self.tight:
            return self.end_first(self.launch(value)) if self.flying or self.waiting else value
        until = self.clock + time
        value = self.catch_up(value, until)
        self.clock = max(self.clock, until)
        return value

    def need(self, value, *chains):
        while any(chain.step == 0 or chain in self.waiting for chain in chains) or any(
            chain is flying for chain in chains for _, flying in self.flying
        ):
            value = self.end_first(self.launch(value))
        return value


class Group:
    def __init__(self, count, belt):
        self.count, self.belt = count, belt
        self.index = lax.axis_index("mp")
        self.bits = [bit for bit in range(count.bit_length() - 1)]

    def side(self, bit):
        return (self.index >> bit) & 1

    def swap(self, value, bit):
        return lax.ppermute(value, "mp", [(i, i ^ (1 << bit)) for i in range(self.count)])

    def own(self, values):
        for bit in self.bits:
            half = values.shape[0] // 2
            values = lax.dynamic_slice_in_dim(values, self.side(bit) * half, half)
        return values

    swap_times = (3.5, 9.5)

    def during(self, value, bit, ticks):
        return self.belt.idle(value, self.swap_times[min(bit, 1)]) if ticks else value

    def scatter(self, terms, ticks=True):
        for bit in self.bits:
            half = terms.shape[0] // 2
            keep = lax.dynamic_slice_in_dim(terms, self.side(bit) * half, half)
            give = lax.dynamic_slice_in_dim(terms, (1 - self.side(bit)) * half, half)
            got = self.swap(give.astype(bf16), bit)
            keep = self.during(keep, bit, ticks)
            terms = keep.astype(f32) + got.astype(f32)
        return terms

    def gather(self, values, ticks=True):
        for bit in reversed(self.bits):
            extent = values.shape[0]
            other = self.swap(values, bit)
            values = self.during(values, bit, ticks)
            whole = jnp.zeros((2 * extent,) + values.shape[1:], values.dtype)
            whole = lax.dynamic_update_slice_in_dim(whole, values, self.side(bit) * extent, 0)
            values = lax.dynamic_update_slice_in_dim(
                whole, other, (1 - self.side(bit)) * extent, 0
            )
        return values

    def total(self, values):
        for bit in self.bits:
            values = values + self.swap(values.astype(bf16), bit).astype(f32)
        return values


def layer_norm(values, gain, shift):
    average = jnp.mean(values, axis=-1, keepdims=True)
    centred = values - average
    variance = jnp.mean(centred * centred, axis=-1, keepdims=True)
    return centred * lax.rsqrt(variance + epsilon) * gain + shift


def layer_norm_pull(values, gain, grad):
    average = jnp.mean(values, axis=-1, keepdims=True)
    centred = values - average
    scale = lax.rsqrt(jnp.mean(centred * centred, axis=-1, keepdims=True) + epsilon)
    unit = centred * scale
    inner = grad * gain
    along = jnp.mean(inner * unit, axis=-1, keepdims=True)
    grad_values = scale * (inner - jnp.mean(inner, axis=-1, keepdims=True) - unit * along)
    return grad_values, jnp.sum(grad * unit, axis=0), jnp.sum(grad, axis=0)


def rotary_tables(length):
    half_width = DH // 2
    frequency = 10000.0 ** (-jnp.arange(half_width, dtype=f32) / half_width)
    angles = jnp.arange(length, dtype=f32)[:, None] * frequency[None, :]
    cosine, sine = jnp.cos(angles), jnp.sin(angles)
    return (
        jnp.concatenate([cosine, cosine], axis=1),
        jnp.concatenate([-sine, sine], axis=1),
    )


def dot(left, right):
    return jnp.dot(left, right, preferred_element_type=f32)


def contract_rows(left, right):
    return lax.dot_general(left, right, (((0,), (0,)), ((), ())), preferred_element_type=f32)


def contract_cols(left, right):
    return lax.dot_general(left, right, (((1,), (1,)), ((), ())), preferred_element_type=f32)


ROWS = 256
short_kernel = pl.CostEstimate(flops=1000, bytes_accessed=1000, transcendentals=0)


def turned(values, cosine, sine):
    return values * cosine + pltpu.roll(values, DH // 2, 1) * sine


def block_probs(query, key, segment_column, segment_row, first):
    scores = contract_cols(query, key) * DH ** (-0.5)
    row = lax.broadcasted_iota(jnp.int32, scores.shape, 0) + first
    column = lax.broadcasted_iota(jnp.int32, scores.shape, 1)
    allowed = (row >= column) & (segment_column == segment_row)
    scores = jnp.where(allowed, scores, masked_value)
    exponent = jnp.exp(scores - jnp.max(scores, axis=-1, keepdims=True))
    return exponent * (1.0 / jnp.sum(exponent, axis=-1, keepdims=True))


def lay_out(pieces, whole, columns=slice(None)):
    start = 0
    for piece in pieces:
        whole[start : start + piece.shape[0], columns] = piece[...]
        start += piece.shape[0]


def pack_kernel(query, key, value, out, pack):
    for first in range(0, query.shape[1], DH):
        for member, source in enumerate((query, key, value, out)):
            place = 4 * first + member * DH
            pack[:, place : place + DH] = source[:, first : first + DH]


def attend_kernel(count, *refs):
    pieces, refs = refs[:count], refs[count:]
    normed, cosine, sine, seg_column, seg_row, *refs = refs
    heads, mixture, terms, normed_t, weight, out_weight, mixtures = refs
    lay_out(pieces, weight)
    step = pl.program_id(0)

    @pl.when(step == 0)
    def _():
        normed_t[...] = normed[...].T

    length = normed.shape[0]
    projected = dot(normed[...], weight[:, : 3 * DH])
    turn = cosine[...], sine[...]
    heads[:, :DH] = turned(projected[:, :DH], *turn).astype(bf16)
    heads[:, DH : 2 * DH] = turned(projected[:, DH : 2 * DH], *turn).astype(bf16)
    heads[:, 2 * DH :] = projected[:, 2 * DH :].astype(bf16)
    for first in range(0, length, ROWS):
        last = first + ROWS
        probs = block_probs(
            heads[first:last, :DH],
            heads[:last, DH : 2 * DH],
            seg_column[first:last, :],
            seg_row[:, :last],
            first,
        )
        mixture[first:last, :] = dot(probs.astype(bf16), heads[:last, 2 * DH :]).astype(bf16)
    place = pl.ds(pl.multiple_of(step * DH, DH), DH)
    out_weight[:, place] = weight[:, 3 * DH :]
    mixtures[:, place] = mixture[...]

    @pl.when(step == pl.num_programs(0) - 1)
    def _():
        terms[...] = contract_cols(mixtures[...], out_weight[...]).astype(bf16)


def attend_pull_kernel(count, *refs):
    pieces, refs = refs[:count], refs[count:]
    grad_attn, normed_t, heads, mixture, cosine, sine, seg_column, seg_row, *refs = refs
    grads, terms, grad_heads, grad_key, grad_value, grad_attn_t, weight, weights, all_grads = refs
    lay_out(pieces, weight)
    step = pl.program_id(0)

    @pl.when(step == 0)
    def _():
        grad_attn_t[...] = grad_attn[...].T

    length = grad_attn.shape[0]
    grad_mixture = dot(grad_attn[...], weight[:, 3 * DH :]).astype(bf16)
    grad_key[...] = jnp.zeros_like(grad_key)
    grad_value[...] = jnp.zeros_like(grad_value)
    scale = DH ** (-0.5)
    for first in range(0, length, ROWS):
        last = first + ROWS
        query = heads[first:last, :DH]
        key = heads[:last, DH : 2 * DH]
        probs = block_probs(query, key, seg_column[first:last, :], seg_row[:, :last], first)
        grad_rows = grad_mixture[first:last]
        grad_probs = contract_cols(grad_rows, heads[:last, 2 * DH :])
        inner = jnp.sum(probs * grad_probs, axis=-1, keepdims=True)
        grad_scores = (probs * (grad_probs - inner)).astype(bf16)
        grad_query = dot(grad_scores, key) * scale
        grad_heads[first:last, :DH] = turned(
            grad_query, cosine[first:last, :], -sine[first:last, :]
        ).astype(bf16)
        grad_key[:last, :] += contract_rows(grad_scores, query)
        grad_value[:last, :] += contract_rows(probs.astype(bf16), grad_rows)
    grad_heads[:, DH : 2 * DH] = turned(
        grad_key[...] * scale, cosine[...], -sine[...]
    ).astype(bf16)
    grad_heads[:, 2 * DH :] = grad_value[...].astype(bf16)
    grads[:, : 3 * DH] = dot(normed_t[...], grad_heads[...]).astype(bf16)
    grads[:, 3 * DH :] = dot(grad_attn_t[...], mixture[...]).astype(bf16)
    place = pl.ds(pl.multiple_of(step * 3 * DH, DH), 3 * DH)
    weights[:, place] = weight[:, : 3 * DH]
    all_grads[:, place] = grad_heads[...]

    @pl.when(step == pl.num_programs(0) - 1)
    def _():
        terms[...] = contract_cols(all_grads[...], weights[...]).astype(bf16)


def fixed(shape):
    return pl.BlockSpec(shape, lambda step: (0, 0))


def first_norm_kernel(values, gain, shift, normed):
    normed[...] = layer_norm(values[...], gain[...], shift[...]).astype(bf16)


def first_norm(values, gain, shift):
    tokens, width = values.shape
    rows = pl.BlockSpec((ROWS, width), lambda step: (step, 0))
    return pl.pallas_call(
        first_norm_kernel,
        grid=(tokens // ROWS,),
        in_specs=[rows, fixed(gain.shape), fixed(shift.shape)],
        out_specs=rows,
        out_shape=jax.ShapeDtypeStruct((tokens, width), bf16),
        cost_estimate=short_kernel,
        name="first_norm",
    )(values, gain, shift)


def by_column(rows, columns):
    return pl.BlockSpec((rows, columns), lambda step: (0, step))


def by_piece(piece, member, columns):
    return pl.BlockSpec((None, piece.shape[1], columns), lambda step: (member, 0, step))


def pack_heads(query, key, value, out, layer):
    share, width = query.shape[1:]
    members = query, key, value, out.transpose(0, 2, 1)
    return pl.pallas_call(
        pack_kernel,
        grid=(1,),
        in_specs=[pl.BlockSpec((None, share, width), lambda step: (layer, 0, 0))] * 4,
        out_specs=pl.BlockSpec((None, share, 4 * width), lambda step: (0, 0, 0)),
        out_shape=jax.ShapeDtypeStruct((1, share, 4 * width), bf16),
        cost_estimate=short_kernel,
        name="pack_heads",
    )(*members)


def attend(normed, pieces, tables):
    tokens, width = normed.shape
    heads = pieces[0].shape[2] // (4 * DH)
    return pl.pallas_call(
        partial(attend_kernel, len(pieces)),
        grid=(heads,),
        in_specs=[
            *[by_piece(piece, 0, 4 * DH) for piece in pieces],
            fixed((tokens, width)),
            *[fixed(table.shape) for table in tables],
        ],
        out_specs=[
            by_column(tokens, 3 * DH),
            by_column(tokens, DH),
            fixed((tokens, width)),
            fixed((width, tokens)),
        ],
        out_shape=[
            jax.ShapeDtypeStruct((tokens, heads * 3 * DH), bf16),
            jax.ShapeDtypeStruct((tokens, heads * DH), bf16),
            jax.ShapeDtypeStruct((tokens, width), bf16),
            jax.ShapeDtypeStruct((width, tokens), bf16),
        ],
        scratch_shapes=[
            pltpu.VMEM((width, 4 * DH), bf16),
            pltpu.VMEM((width, heads * DH), bf16),
            pltpu.VMEM((tokens, heads * DH), bf16),
        ],
        compiler_params=pltpu.CompilerParams(vmem_limit_bytes=40 * 2**20),
        cost_estimate=short_kernel,
        name="attend",
    )(*pieces, normed, *tables)


def attend_pull(grad_attn, normed_t, pieces, heads, mixture, tables):
    tokens, width = grad_attn.shape
    columns = pieces[0].shape[2]
    return pl.pallas_call(
        partial(attend_pull_kernel, len(pieces)),
        grid=(columns // (4 * DH),),
        in_specs=[
            *[by_piece(piece, 0, 4 * DH) for piece in pieces],
            fixed((tokens, width)),
            fixed((width, tokens)),
            by_column(tokens, 3 * DH),
            by_column(tokens, DH),
            *[fixed(table.shape) for table in tables],
        ],
        out_specs=[by_column(width, 4 * DH), fixed((tokens, width))],
        out_shape=[
            jax.ShapeDtypeStruct((width, columns), bf16),
            jax.ShapeDtypeStruct((tokens, width), bf16),
        ],
        scratch_shapes=[
            pltpu.VMEM((tokens, 3 * DH), bf16),
            pltpu.VMEM((tokens, DH), f32),
            pltpu.VMEM((tokens, DH), f32),
            pltpu.VMEM((width, tokens), bf16),
            pltpu.VMEM((width, 4 * DH), bf16),
            pltpu.VMEM((width, columns // 4 * 3), bf16),
            pltpu.VMEM((tokens, columns // 4 * 3), bf16),
        ],
        compiler_params=pltpu.CompilerParams(vmem_limit_bytes=40 * 2**20),
        cost_estimate=short_kernel,
        name="attend_pull",
    )(*pieces, grad_attn, normed_t, heads, mixture, *tables)


def gelu_and_slope(values):
    root = (2.0 / jnp.pi) ** 0.5
    bent = root + (0.044715 * root) * (values * values)
    half = 0.5 + 0.5 * jnp.tanh(values * bent)
    value = values * half
    return value, half + value * (1.0 - half) * (6.0 * bent - 4.0 * root)


UNITS = 512


def add_terms(step, added, total, terms):
    @pl.when(step == 0)
    def _():
        total[...] = added

    @pl.when(step > 0)
    def _():
        total[...] += added

    @pl.when(step == pl.num_programs(0) - 1)
    def _():
        terms[...] = total[...].astype(bf16)


def open_units(second, up, shift, limit, active, slope, second_t):
    @pl.when(pl.program_id(0) == 0)
    def _():
        second_t[...] = second[...].T

    upward = dot(second[...], up[...]) + shift[...]
    value, rise = gelu_and_slope(upward)
    unit = lax.broadcasted_iota(jnp.int32, upward.shape, 1) + pl.program_id(0) * UNITS
    inside = unit < limit[...]
    active[...] = jnp.where(inside, value, 0.0).astype(bf16)
    slope[...] = jnp.where(inside, rise, 0.0).astype(bf16)


def this_cut():
    return pl.ds(pl.multiple_of(pl.program_id(0) * UNITS, UNITS), UNITS)


def units_kernel(count, *refs):
    ups, downs, refs = refs[:count], refs[count : 2 * count], refs[2 * count :]
    second, shift, limit, active, slope, second_t, terms, up, down, all_active = refs
    lay_out(ups, up)
    lay_out(downs, down, this_cut())
    open_units(second, up, shift, limit, active, slope, second_t)
    all_active[:, this_cut()] = active[...]

    @pl.when(pl.program_id(0) == pl.num_programs(0) - 1)
    def _():
        terms[...] = contract_cols(all_active[...], down[...]).astype(bf16)


def last_units_kernel(count, *refs):
    ups, refs = refs[:count], refs[count:]
    second, grad_branch_t, shift, limit, active, slope, second_t, grad_down, up = refs
    lay_out(ups, up)
    open_units(second, up, shift, limit, active, slope, second_t)
    grad_down[...] = dot(grad_branch_t[...], active[...]).astype(bf16)


def units_pull_kernel(count, last, *refs):
    ups, downs, refs = refs[:count], refs[count : 2 * count], refs[2 * count :]
    grad_branch, second_t, slope, active, *refs = refs
    if last:
        grad_up, shift_grad, terms, down, up, all_grads = refs
    else:
        grad_up, grad_down, shift_grad, terms, down, up, all_grads, grad_branch_t = refs
    lay_out(ups, up, this_cut())
    lay_out(downs, down)
    grad_upward = (dot(grad_branch[...], down[...]) * slope[...].astype(f32)).astype(bf16)
    grad_up[...] = dot(second_t[...], grad_upward).astype(bf16)
    shift_grad[...] = jnp.sum(grad_upward.astype(f32), axis=0, keepdims=True)
    all_grads[:, this_cut()] = grad_upward
    if not last:

        @pl.when(pl.program_id(0) == 0)
        def _():
            grad_branch_t[...] = grad_branch[...].T

        grad_down[...] = dot(grad_branch_t[...], active[...]).astype(bf16)

    @pl.when(pl.program_id(0) == pl.num_programs(0) - 1)
    def _():
        terms[...] = contract_cols(all_grads[...], up[...]).astype(bf16)


def units_call(kernel, name, wholes, operands, results, scratch):
    def spec(shape, cut):
        return by_column(shape[0], UNITS) if cut else fixed(shape)

    pieces = [(piece, member) for group, member in wholes for piece in group]
    units = pieces[0][0].shape[2]
    width = sum(piece.shape[1] for piece in wholes[0][0])
    return pl.pallas_call(
        kernel,
        grid=(units // UNITS,),
        in_specs=[
            *[by_piece(piece, member, UNITS) for piece, member in pieces],
            *[spec(part.shape, cut) for part, cut in operands],
        ],
        out_specs=[spec(part.shape, cut) for part, cut in results],
        out_shape=[part for part, _ in results],
        scratch_shapes=[pltpu.VMEM(shape, kind) for shape, kind in scratch],
        compiler_params=pltpu.CompilerParams(vmem_limit_bytes=56 * 2**20),
        cost_estimate=short_kernel,
        name=name,
    )(*[piece for piece, _ in pieces], *[part for part, _ in operands])


def run_units(second, up, down, shift, limit):
    tokens, width = second.shape
    kept = jax.ShapeDtypeStruct((tokens, up[0][0].shape[2]), bf16)
    return units_call(
        partial(units_kernel, len(up[0])),
        "units",
        [up, down],
        [(second, False), (shift, True), (limit, False)],
        [
            (kept, True),
            (kept, True),
            (jax.ShapeDtypeStruct((width, tokens), bf16), False),
            (jax.ShapeDtypeStruct((tokens, width), bf16), False),
        ],
        [((width, UNITS), bf16), ((width, kept.shape[1]), bf16), (kept.shape, bf16)],
    )


def run_last_units(second, up, grad_branch_t, shift, limit):
    tokens, width = second.shape
    units = up[0][0].shape[2]
    kept = jax.ShapeDtypeStruct((tokens, units), bf16)
    return units_call(
        partial(last_units_kernel, len(up[0])),
        "last_units",
        [up],
        [(second, False), (grad_branch_t, False), (shift, True), (limit, False)],
        [
            (kept, True),
            (kept, True),
            (jax.ShapeDtypeStruct((width, tokens), bf16), False),
            (jax.ShapeDtypeStruct((width, units), bf16), True),
        ],
        [((width, UNITS), bf16)],
    )


def branch_kernel(count, *refs):
    downs, (active, terms, total, down) = refs[:count], refs[count:]
    lay_out(downs, down)
    add_terms(pl.program_id(0), contract_cols(active[...], down[...]), total, terms)


def run_branch(active, down):
    tokens, width = active.shape[0], sum(piece.shape[1] for piece in down[0])
    terms = jax.ShapeDtypeStruct((tokens, width), bf16), False
    return units_call(
        partial(branch_kernel, len(down[0])),
        "branch",
        [down],
        [(active, True)],
        [terms],
        [((tokens, width), f32), ((width, UNITS), bf16)],
    )[0]


def run_units_pull(last, grad_branch, second_t, slope, active, up, down):
    tokens, width = grad_branch.shape
    units = up[0][0].shape[2]
    grad = jax.ShapeDtypeStruct((width, units), bf16), True
    shift_grad = jax.ShapeDtypeStruct((1, units), f32), True
    terms = jax.ShapeDtypeStruct((tokens, width), bf16), False
    scratch = [((width, UNITS), bf16), ((width, units), bf16), ((tokens, units), bf16)]
    return units_call(
        partial(units_pull_kernel, len(up[0]), last),
        "units_pull",
        [up, down],
        [(grad_branch, False), (second_t, False), (slope, True), (active, True)],
        [grad, shift_grad, terms] if last else [grad, grad, shift_grad, terms],
        scratch if last else [*scratch, ((width, tokens), bf16)],
    )


def shards(
    hidden,
    segments,
    granular,
    norm_gain,
    norm_bias,
    w_query,
    w_key,
    w_value,
    w_out,
    w_up,
    b_up,
    w_down,
    b_down,
    cotangent,
):
    rows_count = lax.axis_size("rows")
    layers = w_query.shape[0]
    tokens, width = hidden.shape
    seq_count, seq_length = segments.shape
    head_width = w_query.shape[2]
    units = w_up.shape[3]
    share = width // rows_count
    ring = Ring(rows_count)
    belt = Belt(2)
    busy, need = belt.busy, belt.need
    group = Group(lax.axis_size("mp"), belt)

    vector_count = 16
    vectors = Gather(
        ring,
        jnp.concatenate(
            [
                norm_gain.reshape(2 * layers, share),
                norm_bias.reshape(2 * layers, share),
                b_up.reshape(layers, share),
                b_down,
                jnp.zeros((vector_count - 6 * layers, share), bf16),
            ]
        )[None],
    )
    heads_w = [Gather(ring, pack_heads(w_query, w_key, w_value, w_out, 0))]
    belt.add(heads_w[0], vectors)
    (
        hidden,
        cotangent,
        raw_query,
        raw_key,
        raw_value,
        raw_out,
        raw_up,
        raw_down,
    ) = tie(belt.launch(hidden), cotangent, w_query, w_key, w_value, w_out, w_up, w_down)
    belt.flying.reverse()
    features = (ring.owners[:, None] * share + jnp.arange(share)[None, :]).reshape(width)
    turn = (jnp.arange(width)[:, None] == features[None, :]).astype(bf16)
    hidden = dot(hidden, turn)
    position = jnp.arange(seq_count, dtype=segments.dtype)[:, None]
    marks = segments + 4 * position
    tables = tuple(jnp.tile(table, (seq_count, 1)) for table in rotary_tables(seq_length))
    tables += marks.reshape(tokens, 1), marks.reshape(1, tokens)
    limit = (units // 8 * 2**granular)[:, None]
    hidden, limit, *tables = tie(hidden, limit, *tables)

    def pack_units(layer):
        return [raw_up[layer, :, 0], raw_down[layer, 0].T]

    unit_packs = [[jnp.stack(pack_units(layer))] for layer in range(layers - 1)]
    unit_packs.append([part[None] for part in pack_units(layers - 1)])
    head_packs = [
        pack_heads(raw_query, raw_key, raw_value, raw_out, layer) for layer in range(1, layers)
    ]
    raw_cotangent = cotangent
    cotangent = dot(raw_cotangent, turn).astype(bf16)
    cotangent_t = lax.dot_general(
        turn, raw_cotangent, (((0,), (1,)), ((), ())), preferred_element_type=f32
    ).astype(bf16)

    def ring_round(value, *work):
        return tie(belt.end_first(belt.end_first(value)), *work)

    hidden, unit_packs[0][0] = ring_round(hidden, unit_packs[0][0])
    hidden, *head_packs = ring_round(hidden, *head_packs)
    up_w, down_w = [], []
    for layer in range(layers):
        if layer > 0:
            heads_w.append(Gather(ring, head_packs[layer - 1]))
            belt.add(heads_w[layer])
        chains = [Gather(ring, pack) for pack in unit_packs[layer]]
        belt.add(*chains)
        up_w.append((chains[0], 0))
        down_w.append((chains[-1], len(chains) % 2))
    hidden = need(hidden, vectors)
    table = jnp.concatenate([part[0] for part in whole_blocks(vectors.pieces)], axis=1)
    up_shift = contract_cols(table[4 * layers : 5 * layers], turn)
    table = table.astype(f32)
    gains = table[: 2 * layers]
    shifts = table[2 * layers : 4 * layers]
    down_shift = table[5 * layers : 6 * layers]

    state = group.own(hidden)
    normed = first_norm(hidden, gains[:1], shifts[:1])
    def pieces_of(place):
        chain, member = place
        return chain.pieces, member

    kept = []
    for layer in range(layers):
        normed = need(normed, heads_w[layer])
        if layer == 0:
            normed = belt.end_first(normed)
        belt.tight = layer == 0
        heads, mixture, head_terms, normed_t = attend(normed, heads_w[layer].pieces, tables)
        head_terms = busy(head_terms, 10.0)
        middle = state + group.scatter(head_terms)
        belt.clock += 2.5
        second = group.gather(
            layer_norm(middle, gains[2 * layer + 1], shifts[2 * layer + 1]).astype(bf16)
        )
        belt.clock += 2.0
        belt.tight = False
        second = need(second, up_w[layer][0])
        shift = up_shift[layer][None]
        if layer + 1 == layers:
            active, slope, second_t, down_terms = run_last_units(
                second, pieces_of(up_w[layer]), cotangent_t, shift, limit
            )
        else:
            active, slope, second_t, unit_terms = run_units(
                second, pieces_of(up_w[layer]), pieces_of(down_w[layer]), shift, limit
            )
        kept.append((state, normed_t, heads, mixture, middle, second_t, active, slope))
        if layer + 1 < layers:
            unit_terms = busy(unit_terms, 13.0)
            branch = group.scatter(unit_terms) + down_shift[layer]
            belt.clock += 2.5
            state = middle + branch.astype(bf16).astype(f32)
            normed = group.gather(
                layer_norm(state, gains[2 * layer + 2], shifts[2 * layer + 2]).astype(bf16)
            )
            belt.clock += 2.0

    grad_branch = cotangent
    grad_state = group.own(cotangent).astype(f32)
    gain_grads, shift_grads = [None] * (2 * layers), [None] * (2 * layers)
    up_shift_grads, down_shift_grads = [None] * layers, [None] * layers
    heads_g, up_g, down_g = [None] * layers, [None] * layers, [None] * layers
    for layer in reversed(range(layers)):
        layer_input, normed_t, heads, mixture, middle, second_t, active, slope = kept[layer]
        last = layer + 1 == layers
        down_shift_grads[layer] = jnp.sum(grad_branch.astype(f32), axis=0)
        if last:
            active = busy(active, 12.0)
            active = need(active, down_w[layer][0])
        pulled = run_units_pull(
            last,
            grad_branch,
            second_t,
            slope,
            active,
            pieces_of(up_w[layer]),
            pieces_of(down_w[layer]),
        )
        if last:
            up_terms, shift_grad, unit_terms = pulled
            result = middle, active
        else:
            up_terms, down_terms, shift_grad, unit_terms = pulled
        chain = Scatter(ring, up_terms, down_terms)
        up_g[layer], down_g[layer] = (chain, 0), (chain, 1)
        up_shift_grads[layer] = shift_grad[0]
        belt.add(chain)
        unit_terms = busy(unit_terms, 16.0)
        grad_second = group.scatter(unit_terms)
        grad_second = grad_second.astype(bf16).astype(f32)
        pulled, gain_grads[2 * layer + 1], shift_grads[2 * layer + 1] = layer_norm_pull(
            middle, gains[2 * layer + 1], grad_second
        )
        belt.clock += 3.0
        grad_middle = grad_state + pulled
        grad_attn = group.gather(grad_middle.astype(bf16))
        belt.clock += 2.0
        head_terms, grad_terms = attend_pull(
            grad_attn, normed_t, heads_w[layer].pieces, heads, mixture, tables
        )
        if layer > 0:
            heads_g[layer] = Scatter(ring, head_terms)
            belt.add(heads_g[layer])
        grad_terms = busy(grad_terms, 18.0)
        belt.tight = layer == 0
        grad_normed = group.scatter(grad_terms)
        pulled, gain_grads[2 * layer], shift_grads[2 * layer] = layer_norm_pull(
            layer_input, gains[2 * layer], grad_normed
        )
        belt.clock += 3.0
        grad_state = grad_middle + pulled
        if layer > 0:
            grad_branch = group.gather(grad_state.astype(bf16))
            belt.clock += 2.0

    norm_parts = group.total(jnp.stack(gain_grads + shift_grads)).astype(bf16)
    vector_parts = jnp.concatenate(
        [
            norm_parts,
            dot(jnp.stack(up_shift_grads).astype(bf16), turn).astype(bf16),
            jnp.stack(down_shift_grads).astype(bf16),
            jnp.zeros((vector_count - 6 * layers, width), bf16),
        ]
    )
    vector_parts = vector_parts.reshape(vector_count, rows_count, share).transpose(1, 0, 2)
    columns = head_terms.shape[1]
    last_terms = jnp.concatenate(
        [
            head_terms.reshape(rows_count, share, columns),
            jnp.pad(vector_parts, ((0, 0), (0, 0), (0, columns - share))),
        ],
        axis=1,
    ).reshape(-1, columns)
    grad_state, last_terms = tie(grad_state, last_terms)
    heads_g[0] = Scatter(ring, last_terms)
    belt.add(heads_g[0])
    grad_hidden = contract_cols(group.gather(grad_state.astype(bf16)), turn)
    middle, active, grad_hidden = tie(*result, grad_hidden)
    unit_terms = run_branch(active, pieces_of(down_w[-1]))
    state = middle + (group.scatter(unit_terms) + down_shift[-1]).astype(bf16).astype(f32)
    result = contract_cols(group.gather(state.astype(bf16)), turn).astype(bf16)
    chains = [*heads_g, *(chain for chain, _ in up_g + down_g)]
    result = need(result, *chains)
    vector_sums = heads_g[0].total[0, share:, :share]

    def member_grad(chain, member):
        return jnp.concatenate(
            [
                chain.total[0, :share, first + member * DH : first + (member + 1) * DH]
                for first in range(0, 4 * head_width, 4 * DH)
            ],
            axis=1,
        )

    query_grad, key_grad, value_grad, out_grad = (
        [member_grad(chain, member) for chain in heads_g] for member in range(4)
    )
    return (
        result,
        grad_hidden,
        vector_sums[: 2 * layers].reshape(layers, 2, share),
        vector_sums[2 * layers : 4 * layers].reshape(layers, 2, share),
        jnp.stack(query_grad),
        jnp.stack(key_grad),
        jnp.stack(value_grad),
        jnp.stack([part.T for part in out_grad]),
        jnp.stack([chain.total[member] for chain, member in up_g])[:, :, None],
        vector_sums[4 * layers : 5 * layers][:, None],
        jnp.stack([chain.total[member].T for chain, member in down_g])[:, None],
        vector_sums[5 * layers : 6 * layers],
    )


def solution(mesh):
    return jax.shard_map(
        shards,
        mesh=mesh,
        in_specs=(
            P("rows", None),
            P("rows", None),
            P("rows"),
            P(None, None, "rows"),
            P(None, None, "rows"),
            P(None, "rows", "mp"),
            P(None, "rows", "mp"),
            P(None, "rows", "mp"),
            P(None, "mp", "rows"),
            P(None, "rows", "mp", None),
            P(None, "mp", "rows"),
            P(None, "mp", None, "rows"),
            P(None, "rows"),
            P("rows", None),
        ),
        out_specs=(
            P("rows", None),
            P("rows", None),
            P(None, None, "rows"),
            P(None, None, "rows"),
            P(None, "rows", "mp"),
            P(None, "rows", "mp"),
            P(None, "rows", "mp"),
            P(None, "mp", "rows"),
            P(None, "rows", "mp", None),
            P(None, "mp", "rows"),
            P(None, "mp", None, "rows"),
            P(None, "rows"),
        ),
        check_vma=False,
    )
```

time: 2750 us -> 679 us (0.25)
  waiting for transfers between devices: 1710 us -> 273 us
  blocking collectives: 322 us -> 0 us
  local copies, waits for them, and re-layouts: 367 us -> 73.1 us
  Pallas kernels: 0 us -> 125 us
  matrix products: 120 us -> 26.2 us
  starting transfers between devices: 38.9 us -> 103 us
  loops' own time: 47 us -> 0 us
  other arithmetic: 107 us -> 65.3 us
    unnamed x27 -> x0, waiting for transfers between devices: 565 us -> none
    psum x7 -> x0, waiting for transfers between devices: 402 us -> none  [the longest x4 281 us: send_back(): lax.psum(as_sent(terms), 'mp')]
    reduce_scatter x4 -> x0, waiting for transfers between devices: 369 us -> none  [the longest x1 159 us: shards(): lax.psum_scatter(stacked[8].astype(jnp.bfloat16), 'rows', scatter_dimensi...]
    ppermute x0 -> x114, waiting for transfers between devices: none -> 273 us  [the longest x40 202 us: ahead(): return lax.ppermute(value, 'rows', self.pairs)]
    all_gather x4 -> x0, blocking collectives: 246 us -> none  [the longest x1 157 us: shards(): lax.all_gather(b_up, 'rows', axis=2, tiled=True)]
    all_gather x6 -> x0, waiting for transfers between devices: 197 us -> none  [the longest x1 97.4 us: shards(): lax.all_gather(w_up, 'rows', axis=1, tiled=True)]
    all_to_all x7 -> x0, waiting for transfers between devices: 178 us -> none  [the longest x4 127 us: send_back(): lax.all_to_all(total.reshape(rows_count, slot_rows, width), 'rows', split...]
    slice x8 -> x21, local copies, waits for them, and re-layouts: 145 us -> 9.47 us  [the longest x6 3.49 us: start(): self.forward[:, :half]]
  transfers between devices with their start and end apart: 29 -> 114, of which waited for: 24 -> 67; matrix products, arithmetic and copies ran while one was open for 15% -> 21% of each run, Pallas kernels for 0% -> 16%
where the time goes in v1:
time: 679 us; the launch traced here: 669 us
  waiting for transfers between devices  273 us (40%)
  Pallas kernels  125 us (18%)
  starting transfers between devices  103 us (15%)
  local copies, waits for them, and re-layouts  73.1 us (11%)
  other arithmetic  65.3 us (10%)
  matrix products  26.2 us (4%)
    ppermute x40, waiting for transfers between devices, ahead(): return lax.ppermute(value, 'rows', self.pairs)  202 us
    pallas_call x5, Pallas kernels, units_call(): pl.pallas_call(kernel, grid=(units // UNITS,), in_specs=[*[by_piece(piece...  65 us
    ppermute x40, starting transfers between devices, ahead(): return lax.ppermute(value, 'rows', self.pairs)  43.5 us
    ppermute x34, waiting for transfers between devices, swap(): lax.ppermute(value, 'mp', [(i, i ^ 1 << bit) for i in range(self.count)])  43.3 us
    ppermute x40, starting transfers between devices, back(): return lax.ppermute(value, 'rows', [(b, a) for a, b in self.pairs])  40.8 us
    pallas_call x2, Pallas kernels, attend_pull(): pl.pallas_call(partial(attend_pull_kernel, len(pieces)), grid=(columns //...  33.9 us
    ppermute x40, waiting for transfers between devices, back(): return lax.ppermute(value, 'rows', [(b, a) for a, b in self.pairs])  27.4 us
    unnamed x235, local copies, waits for them, and re-layouts  19.2 us
  transfers between devices with their start and end apart: 114, of which 67 were waited for; matrix products, arithmetic and copies ran while one was open for 21% of the time, Pallas kernels for 16%

profile of v1, /device:TPU:0, one launch (start us, length us, event | category | flops | bytes accessed | tf_op | source)
XLA Modules:
  0.0 668.9 jit_solution(5439919020930592855)
XLA Ops:
  0.7 2.1 pack_heads.2.refs_0_
  3.0 3.1 collective-permute-start
  6.1 2.0 collective-permute-start.2
  11.2 5.8 fusion.7.values
  18.2 2.8 collective-permute-done.2.refs_8_
  28.7 7.3 %collective-permute-done.4 = bf16[1,16,192]{2,1,0:T(8,128)(2,1)S(1)} collective-permute-done((bf16[1,16,192]{2,1,0:T(8,128)(2,1)}, bf16[1,16,192]{2,1,0:T(8,128)(2,1)S(1)}, u32[]{:S(2)}, u32[]{:S(2)}) %collective-permute-start.4) | collective-permute-done | bytes 6176 | tf_op jit(solution)/shard_map/ppermute | solution.py:48
  41.4 2.0 pack_heads.3.refs_0_
  43.4 6.5 collective-permute-done.8
  62.0 3.4 first_norm.1.refs_9_
  65.4 23.2 %collective-permute-done.14.refs_4_ = bf16[1,96,1536]{2,1,0:T(8,128)(2,1)} collective-permute-done((bf16[1,96,1536]{2,1,0:T(8,128)(2,1)}, bf16[1,96,1536]{2,1,0:T(8,128)(2,1)}, u32[]{:S(2)}, u32[]{:S(2)}) %collective-permute-start.14) | collective-permute-done | bytes 294944 | tf_op jit(solution)/shard_map/ppermute | solution.py:48
  99.1 9.3 %attend.2 = (bf16[512,1152]{1,0:T(8,128)(2,1)S(1)}, bf16[512,384]{1,0:T(8,128)(2,1)S(1)}, bf16[512,1536]{1,0:T(8,128)(2,1)S(1)}, bf16[1536,512]{1,0:T(8,128)(2,1)S(1)}) custom-call(bf16[1,192,1536]{2,1,0:T(8,128)(2,1)S(1)} %copy-done.3, bf16[1,192,1536]{2,1,0:T(8,128)(2,1)S(1)} %copy-done.15, bf16[1,192,1536]{2,1,0:T(8,128)(2,1)} %collective-permute-done.7.refs_2_, ...), custom_call_target="tpu_custom_call" | custom-call | flops 1000 | bytes 1000 | tf_op jit(solution)/shard_map/attend/pallas_call | solution.py:458
  114.1 15.7 %collective-permute-done.20.refs_7_.refs_16_ = bf16[2,192,1536]{2,1,0:T(8,128)(2,1)} collective-permute-done((bf16[2,192,1536]{2,1,0:T(8,128)(2,1)}, bf16[2,192,1536]{2,1,0:T(8,128)(2,1)}, u32[]{:S(2)}, u32[]{:S(2)}) %collective-permute-start.20) | collective-permute-done | bytes 1179680 | tf_op jit(solution)/shard_map/ppermute | solution.py:48
  134.5 5.4 collective-permute-done.23.refs_7_
  143.9 2.0 fusion.83
  150.0 17.6 %collective-permute-done.26.refs_6_.refs_15_ = bf16[2,192,1536]{2,1,0:T(8,128)(2,1)S(1)} collective-permute-done((bf16[2,192,1536]{2,1,0:T(8,128)(2,1)}, bf16[2,192,1536]{2,1,0:T(8,128)(2,1)S(1)}, u32[]{:S(2)}, u32[]{:S(2)}) %collective-permute-start.26) | collective-permute-done | bytes 1179680 | tf_op jit(solution)/shard_map/ppermute | solution.py:48
  180.0 8.6 %collective-permute-done.32.refs_4_.refs_13_ = bf16[2,96,1536]{2,1,0:T(8,128)(2,1)} collective-permute-done((bf16[2,96,1536]{2,1,0:T(8,128)(2,1)}, bf16[2,96,1536]{2,1,0:T(8,128)(2,1)}, u32[]{:S(2)}, u32[]{:S(2)}) %collective-permute-start.32) | collective-permute-done | bytes 589856 | tf_op jit(solution)/shard_map/ppermute | solution.py:48
  195.4 13.4 %units.1 = (bf16[512,1536]{1,0:T(8,128)(2,1)}, bf16[512,1536]{1,0:T(8,128)(2,1)}, bf16[1536,512]{1,0:T(8,128)(2,1)}, bf16[512,1536]{1,0:T(8,128)(2,1)}) custom-call(bf16[2,192,1536]{2,1,0:T(8,128)(2,1)} %pad_maximum_fusion.refs_0_.refs_9_, bf16[2,192,1536]{2,1,0:T(8,128)(2,1)} %collective-permute-done.17.refs_1_.refs_10_, ...), custom_call_target="tpu_custom_call" | custom-call | flops 1000 | bytes 1000 | tf_op jit(solution)/shard_map/units/pallas_call | solution.py:619
  219.2 8.8 %collective-permute-done.39.refs_17_.refs_8_ = bf16[1,192,1536]{2,1,0:T(8,128)(2,1)S(1)} collective-permute-done((bf16[1,192,1536]{2,1,0:T(8,128)(2,1)S(1)}, bf16[1,192,1536]{2,1,0:T(8,128)(2,1)S(1)}, u32[]{:S(2)}, u32[]{:S(2)}) %collective-permute-start.39) | collective-permute-done | bytes 589856 | tf_op jit(solution)/shard_map/ppermute | solution.py:48
  231.2 8.9 %collective-permute-done.42.refs_7_ = bf16[1,192,1536]{2,1,0:T(8,128)(2,1)S(1)} collective-permute-done((bf16[1,192,1536]{2,1,0:T(8,128)(2,1)}, bf16[1,192,1536]{2,1,0:T(8,128)(2,1)S(1)}, u32[]{:S(2)}, u32[]{:S(2)}) %collective-permute-start.42) | collective-permute-done | bytes 589856 | tf_op jit(solution)/shard_map/ppermute | solution.py:48
  241.3 1.9 collective-permute-start.47
  243.4 9.5 %attend.3 = (bf16[512,1152]{1,0:T(8,128)(2,1)S(1)}, bf16[512,384]{1,0:T(8,128)(2,1)S(1)}, bf16[512,1536]{1,0:T(8,128)(2,1)S(1)}, bf16[1536,512]{1,0:T(8,128)(2,1)S(1)}) custom-call(bf16[1,192,1536]{2,1,0:T(8,128)(2,1)S(1)} %copy-done.4, bf16[1,192,1536]{2,1,0:T(8,128)(2,1)} %collective-permute-done.19.refs_1_, ...), custom_call_target="tpu_custom_call" | custom-call | flops 1000 | bytes 1000 | tf_op jit(solution)/shard_map/attend/pallas_call | solution.py:458
  253.0 3.4 collective-permute-done.46.refs_16_.refs_7_
  263.4 10.0 %collective-permute-done.49.refs_6_ = bf16[1,192,1536]{2,1,0:T(8,128)(2,1)S(1)} collective-permute-done((bf16[1,192,1536]{2,1,0:T(8,128)(2,1)S(1)}, bf16[1,192,1536]{2,1,0:T(8,128)(2,1)S(1)}, u32[]{:S(2)}, u32[]{:S(2)}) %collective-permute-start.49) | collective-permute-done | bytes 589856 | tf_op jit(solution)/shard_map/ppermute | solution.py:48
  279.4 3.8 fusion.18.refs_10_
  283.2 2.9 collective-permute-done.52.refs_15_.refs_6_
  289.1 2.8 collective-permute-done.54.refs_4_
  293.5 4.5 fusion.87
  301.6 11.8 %last_units.1 = (bf16[512,1536]{1,0:T(8,128)(2,1)}, bf16[512,1536]{1,0:T(8,128)(2,1)}, bf16[1536,512]{1,0:T(8,128)(2,1)}, bf16[1536,1536]{1,0:T(8,128)(2,1)}) custom-call(bf16[1,192,1536]{2,1,0:T(8,128)(2,1)} %get-tuple-element.347.refs_0_, bf16[1,192,1536]{2,1,0:T(8,128)(2,1)} %collective-permute-done.37.refs_1_, bf16[1,192,1536]{2,1,0:T(8,128)(2,1)} %copy-done.54, ...), custom_call_target="tpu_custom_call" | custom-call | flops 1000 | bytes 1000 | tf_op jit(solution)/shard_map/last_units/pallas_call | solution.py:619
  313.4 14.5 %units_pull.2 = (bf16[1536,1536]{1,0:T(8,128)(2,1)}, f32[1,1536]{1,0:T(1,128)}, bf16[512,1536]{1,0:T(8,128)(2,1)}) custom-call(bf16[1,192,1536]{2,1,0:T(8,128)(2,1)} %get-tuple-element.347.refs_0_, bf16[1,192,1536]{2,1,0:T(8,128)(2,1)} %collective-permute-done.37.refs_1_, bf16[1,192,1536]{2,1,0:T(8,128)(2,1)} %copy-done.54, ...), custom_call_target="tpu_custom_call" | custom-call | flops 1000 | bytes 1000 | tf_op jit(solution)/shard_map/units_pull/pallas_call | solution.py:619
  338.2 6.3 collective-permute-done.61
  348.0 3.2 collective-permute-done.62
  357.1 2.1 collective-permute-done.65
  359.3 17.0 %attend_pull.2 = (bf16[1536,1536]{1,0:T(8,128)(2,1)}, bf16[512,1536]{1,0:T(8,128)(2,1)S(1)}) custom-call(bf16[1,192,1536]{2,1,0:T(8,128)(2,1)S(1)} %copy-done.4, bf16[1,192,1536]{2,1,0:T(8,128)(2,1)} %collective-permute-done.19.refs_1_, bf16[1,192,1536]{2,1,0:T(8,128)(2,1)} %collective-permute-done.24.refs_2_, ...), custom_call_target="tpu_custom_call" | custom-call | flops 1000 | bytes 1000 | tf_op jit(solution)/shard_map/attend_pull/pallas_call | solution.py:492
  376.3 3.2 collective-permute-done.66
  381.6 1.7 copy-done.39
  390.9 9.7 %collective-permute-done.69 = bf16[128,1536]{1,0:T(8,128)(2,1)S(1)} collective-permute-done((bf16[128,1536]{1,0:T(8,128)(2,1)S(1)}, bf16[128,1536]{1,0:T(8,128)(2,1)S(1)}, u32[]{:S(2)}, u32[]{:S(2)}) %collective-permute-start.69) | collective-permute-done | bytes 393248 | tf_op jit(solution)/shard_map/ppermute | solution.py:215
  402.8 11.8 %collective-permute-done.70 = bf16[2,192,1536]{2,1,0:T(8,128)(2,1)S(1)} collective-permute-done((bf16[2,192,1536]{2,1,0:T(8,128)(2,1)S(1)}, bf16[2,192,1536]{2,1,0:T(8,128)(2,1)S(1)}, u32[]{:S(2)}, u32[]{:S(2)}) %collective-permute-start.70) | collective-permute-done | bytes 1179680 | tf_op jit(solution)/shard_map/ppermute | solution.py:48
  427.6 18.1 %units_pull.3 = (bf16[1536,1536]{1,0:T(8,128)(2,1)}, bf16[1536,1536]{1,0:T(8,128)(2,1)}, f32[1,1536]{1,0:T(1,128)}, bf16[512,1536]{1,0:T(8,128)(2,1)}) custom-call(bf16[2,192,1536]{2,1,0:T(8,128)(2,1)} %pad_maximum_fusion.refs_0_.refs_9_, bf16[2,192,1536]{2,1,0:T(8,128)(2,1)} %collective-permute-done.17.refs_1_.refs_10_, ...), custom_call_target="tpu_custom_call" | custom-call | flops 1000 | bytes 1000 | tf_op jit(solution)/shard_map/units_pull/pallas_call | solution.py:619
  448.8 3.9 slice_bitcast_fusion.7
  458.1 2.1 convert_add_fusion
  461.2 2.6 fusion.40
  463.8 7.7 %collective-permute-done.81 = bf16[128,1536]{1,0:T(8,128)(2,1)S(1)} collective-permute-done((bf16[128,1536]{1,0:T(8,128)(2,1)S(1)}, bf16[128,1536]{1,0:T(8,128)(2,1)S(1)}, u32[]{:S(2)}, u32[]{:S(2)}) %collective-permute-start.81) | collective-permute-done | bytes 393248 | tf_op jit(solution)/shard_map/ppermute | solution.py:215
  478.2 5.2 collective-permute-done.84
  487.8 2.3 fusion.27
  497.9 16.9 %attend_pull.3 = (bf16[1536,1536]{1,0:T(8,128)(2,1)}, bf16[512,1536]{1,0:T(8,128)(2,1)S(1)}) custom-call(bf16[1,192,1536]{2,1,0:T(8,128)(2,1)S(1)} %copy-done.3, bf16[1,192,1536]{2,1,0:T(8,128)(2,1)S(1)} %copy-done.16, bf16[1,192,1536]{2,1,0:T(8,128)(2,1)} %collective-permute-done.7.refs_2_, bf16[1,192,1536]{2,1,0:T(8,128)(2,1)S(1)} %copy-done.10, ...), custom_call_target="tpu_custom_call" | custom-call | flops 1000 | bytes 1000 | tf_op jit(solution)/shard_map/attend_pull/pallas_call | solution.py:492
  514.8 1.9 fusion.38
  516.8 10.1 %collective-permute-done.88 = bf16[2,192,1536]{2,1,0:T(8,128)(2,1)S(1)} collective-permute-done((bf16[2,192,1536]{2,1,0:T(8,128)(2,1)}, bf16[2,192,1536]{2,1,0:T(8,128)(2,1)S(1)}, u32[]{:S(2)}, u32[]{:S(2)}) %collective-permute-start.88) | collective-permute-done | bytes 1179680 | tf_op jit(solution)/shard_map/ppermute | solution.py:48
  534.6 11.7 %collective-permute-done.91 = bf16[1,192,1536]{2,1,0:T(8,128)(2,1)S(1)} collective-permute-done((bf16[1,192,1536]{2,1,0:T(8,128)(2,1)S(1)}, bf16[1,192,1536]{2,1,0:T(8,128)(2,1)S(1)}, u32[]{:S(2)}, u32[]{:S(2)}) %collective-permute-start.91) | collective-permute-done | bytes 589856 | tf_op jit(solution)/shard_map/ppermute | solution.py:48
  552.0 4.8 collective-permute-done.93
  562.0 1.8 collective-permute-done.95
  564.1 2.8 fusion.8
  567.5 3.8 collective-permute-done.96
  571.8 2.6 add_convert_fusion
  574.5 2.6 add_convert_fusion.1
  581.6 6.3 collective-permute-done.100
  593.2 4.3 fusion.2
  597.5 7.1 %branch.1 = bf16[512,1536]{1,0:T(8,128)(2,1)} custom-call(bf16[1,192,1536]{2,1,0:T(8,128)(2,1)} %get-tuple-element.349.refs_9_.refs_0_, bf16[1,192,1536]{2,1,0:T(8,128)(2,1)} %copy-done.63, bf16[1,192,1536]{2,1,0:T(8,128)(2,1)} %copy-done.65, bf16[1,192,1536]{2,1,0:T(8,128)(2,1)} %copy-done.46, ...), custom_call_target="tpu_custom_call" | custom-call | flops 1000 | bytes 1000 | tf_op jit(solution)/shard_map/branch/pallas_call | solution.py:619
  606.2 7.4 %collective-permute-done.102 = bf16[2,192,1536]{2,1,0:T(8,128)(2,1)} collective-permute-done((bf16[2,192,1536]{2,1,0:T(8,128)(2,1)}, bf16[2,192,1536]{2,1,0:T(8,128)(2,1)}, u32[]{:S(2)}, u32[]{:S(2)}) %collective-permute-start.102) | collective-permute-done | bytes 1179680 | tf_op jit(solution)/shard_map/ppermute | solution.py:48
  613.6 2.0 convert_add_fusion.1
  616.2 9.4 %collective-permute-done.105 = bf16[1,208,1536]{2,1,0:T(8,128)(2,1)} collective-permute-done((bf16[1,208,1536]{2,1,0:T(8,128)(2,1)}, bf16[1,208,1536]{2,1,0:T(8,128)(2,1)}, u32[]{:S(2)}, u32[]{:S(2)}) %collective-permute-start.105) | collective-permute-done | bytes 639008 | tf_op jit(solution)/shard_map/ppermute | solution.py:48
  630.1 3.8 copy.38
  635.9 6.5 collective-permute-done.108
  646.9 9.5 %collective-permute-done.111 = bf16[1,208,1536]{2,1,0:T(8,128)(2,1)S(1)} collective-permute-done((bf16[1,208,1536]{2,1,0:T(8,128)(2,1)S(1)}, bf16[1,208,1536]{2,1,0:T(8,128)(2,1)S(1)}, u32[]{:S(2)}, u32[]{:S(2)}) %collective-permute-start.111) | collective-permute-done | bytes 639008 | tf_op jit(solution)/shard_map/ppermute | solution.py:48
  664.8 3.8 fusion.22
  (669 shorter events, 236.1 us)
Async XLA Ops:
  37.3 16.0 %collective-permute-start.10 = (bf16[1,192,1536]{2,1,0:T(8,128)(2,1)}, bf16[1,192,1536]{2,1,0:T(8,128)(2,1)S(1)}, u32[]{:S(2)}, u32[]{:S(2)}) collective-permute-start(bf16[1,192,1536]{2,1,0:T(8,128)(2,1)} %collective-permute-done.6.refs_7_), channel_id=1, source_target_pairs={{0,8},{8,16},{16,24},{24,28},{28,20},{20,12},{12,4},{4,0},{1,9},{9... | collective-permute-start | bytes 1769480 | tf_op jit(solution)/shard_map/ppermute | solution.py:48
  56.5 34.8 %collective-permute-start.16 = (bf16[2,192,1536]{2,1,0:T(8,128)(2,1)}, bf16[2,192,1536]{2,1,0:T(8,128)(2,1)}, u32[]{:S(2)}, u32[]{:S(2)}) collective-permute-start(bf16[2,192,1536]{2,1,0:T(8,128)(2,1)} %pad_maximum_fusion.refs_0_.refs_9_), channel_id=1, source_target_pairs={{0,8},{8,16},{16,24},{24,28},{28,20},{20,12},{12,4},{4,0},{1,9},{9... | collective-permute-start | bytes 3538952 | tf_op jit(solution)/shard_map/ppermute | solution.py:48
  57.2 34.0 %collective-permute-start.17 = (bf16[2,192,1536]{2,1,0:T(8,128)(2,1)}, bf16[2,192,1536]{2,1,0:T(8,128)(2,1)}, u32[]{:S(2)}, u32[]{:S(2)}) collective-permute-start(bf16[2,192,1536]{2,1,0:T(8,128)(2,1)} %pad_maximum_fusion.refs_0_.refs_9_), channel_id=1, source_target_pairs={{8,0},{16,8},{24,16},{28,24},{20,28},{12,20},{4,12},{0,4},{9,1},{1... | collective-permute-start | bytes 3538952 | tf_op jit(solution)/shard_map/ppermute | solution.py:51
  58.5 30.1 %collective-permute-start.14 = (bf16[1,96,1536]{2,1,0:T(8,128)(2,1)}, bf16[1,96,1536]{2,1,0:T(8,128)(2,1)}, u32[]{:S(2)}, u32[]{:S(2)}) collective-permute-start(bf16[1,96,1536]{2,1,0:T(8,128)(2,1)} %slice.457), channel_id=1, source_target_pairs={{0,8},{8,16},{16,24},{24,28},{28,20},{20,12},{12,4},{4,0},{1,9},{9... | collective-permute-start | bytes 884744 | tf_op jit(solution)/shard_map/ppermute | solution.py:48
  59.3 30.0 %collective-permute-start.15 = (bf16[1,96,1536]{2,1,0:T(8,128)(2,1)}, bf16[1,96,1536]{2,1,0:T(8,128)(2,1)}, u32[]{:S(2)}, u32[]{:S(2)}) collective-permute-start(bf16[1,96,1536]{2,1,0:T(8,128)(2,1)} %slice.458), channel_id=1, source_target_pairs={{8,0},{16,8},{24,16},{28,24},{20,28},{12,20},{4,12},{0,4},{9,1},{1... | collective-permute-start | bytes 884744 | tf_op jit(solution)/shard_map/ppermute | solution.py:51
  89.2 19.3 %collective-permute-start.18 = (bf16[1,192,1536]{2,1,0:T(8,128)(2,1)S(1)}, bf16[1,192,1536]{2,1,0:T(8,128)(2,1)}, u32[]{:S(2)}, u32[]{:S(2)}) collective-permute-start(bf16[1,192,1536]{2,1,0:T(8,128)(2,1)S(1)} %copy-done.4), channel_id=1, source_target_pairs={{0,8},{8,16},{16,24},{24,28},{28,20},{20,12},{12,4},{4,0},{1,9},{9... | collective-permute-start | bytes 1769480 | tf_op jit(solution)/shard_map/ppermute | solution.py:48
  90.0 18.5 %collective-permute-start.19 = (bf16[1,192,1536]{2,1,0:T(8,128)(2,1)S(1)}, bf16[1,192,1536]{2,1,0:T(8,128)(2,1)}, u32[]{:S(2)}, u32[]{:S(2)}) collective-permute-start(bf16[1,192,1536]{2,1,0:T(8,128)(2,1)S(1)} %copy-done.4), channel_id=1, source_target_pairs={{8,0},{16,8},{24,16},{28,24},{20,28},{12,20},{4,12},{0,4},{9,1},{1... | collective-permute-start | bytes 1769480 | tf_op jit(solution)/shard_map/ppermute | solution.py:51
  91.3 38.6 %collective-permute-start.20 = (bf16[2,192,1536]{2,1,0:T(8,128)(2,1)}, bf16[2,192,1536]{2,1,0:T(8,128)(2,1)}, u32[]{:S(2)}, u32[]{:S(2)}) collective-permute-start(bf16[2,192,1536]{2,1,0:T(8,128)(2,1)} %collective-permute-done.16.refs_8_.refs_17_), channel_id=1, source_target_pairs={{0,8},{8,16},{16,24},{24,28},{28,20},{20,12},{12,4},{4,0},{1,9},{9... | collective-permute-start | bytes 3538952 | tf_op jit(solution)/shard_map/ppermute | solution.py:48
  92.1 38.4 %collective-permute-start.21 = (bf16[2,192,1536]{2,1,0:T(8,128)(2,1)}, bf16[2,192,1536]{2,1,0:T(8,128)(2,1)}, u32[]{:S(2)}, u32[]{:S(2)}) collective-permute-start(bf16[2,192,1536]{2,1,0:T(8,128)(2,1)} %collective-permute-done.17.refs_1_.refs_10_), channel_id=1, source_target_pairs={{8,0},{16,8},{24,16},{28,24},{20,28},{12,20},{4,12},{0,4},{9,1},{1... | collective-permute-start | bytes 3538952 | tf_op jit(solution)/shard_map/ppermute | solution.py:51
  110.7 19.8 %collective-permute-start.22 = (bf16[256,1536]{1,0:T(8,128)(2,1)}, bf16[256,1536]{1,0:T(8,128)(2,1)}, u32[]{:S(2)}, u32[]{:S(2)}) collective-permute-start(bf16[256,1536]{1,0:T(8,128)(2,1)} %get-tuple-element.632), channel_id=1, source_target_pairs={{0,1},{1,0},{2,3},{3,2},{4,5},{5,4},{6,7},{7,6},{8,9},{9,8},{10,11... | collective-permute-start | bytes 2359304 | tf_op jit(solution)/shard_map/ppermute | solution.py:215
  112.0 27.9 %collective-permute-start.23 = (bf16[1,192,1536]{2,1,0:T(8,128)(2,1)}, bf16[1,192,1536]{2,1,0:T(8,128)(2,1)}, u32[]{:S(2)}, u32[]{:S(2)}) collective-permute-start(bf16[1,192,1536]{2,1,0:T(8,128)(2,1)} %collective-permute-done.18.refs_8_), channel_id=1, source_target_pairs={{0,8},{8,16},{16,24},{24,28},{28,20},{20,12},{12,4},{4,0},{1,9},{9... | collective-permute-start | bytes 1769480 | tf_op jit(solution)/shard_map/ppermute | solution.py:48
  112.9 27.5 %collective-permute-start.24 = (bf16[1,192,1536]{2,1,0:T(8,128)(2,1)}, bf16[1,192,1536]{2,1,0:T(8,128)(2,1)}, u32[]{:S(2)}, u32[]{:S(2)}) collective-permute-start(bf16[1,192,1536]{2,1,0:T(8,128)(2,1)} %collective-permute-done.19.refs_1_), channel_id=1, source_target_pairs={{8,0},{16,8},{24,16},{28,24},{20,28},{12,20},{4,12},{0,4},{9,1},{1... | collective-permute-start | bytes 1769480 | tf_op jit(solution)/shard_map/ppermute | solution.py:51
  140.4 27.2 %collective-permute-start.26 = (bf16[2,192,1536]{2,1,0:T(8,128)(2,1)}, bf16[2,192,1536]{2,1,0:T(8,128)(2,1)S(1)}, u32[]{:S(2)}, u32[]{:S(2)}) collective-permute-start(bf16[2,192,1536]{2,1,0:T(8,128)(2,1)} %collective-permute-done.20.refs_7_.refs_16_), channel_id=1, source_target_pairs={{0,8},{8,16},{16,24},{24,28},{28,20},{20,12},{12,4},{4,0},{1,9},{9... | collective-permute-start | bytes 3538952 | tf_op jit(solution)/shard_map/ppermute | solution.py:48
  141.2 27.1 %collective-permute-start.27 = (bf16[2,192,1536]{2,1,0:T(8,128)(2,1)}, bf16[2,192,1536]{2,1,0:T(8,128)(2,1)S(1)}, u32[]{:S(2)}, u32[]{:S(2)}) collective-permute-start(bf16[2,192,1536]{2,1,0:T(8,128)(2,1)} %collective-permute-done.21.refs_2_.refs_11_), channel_id=1, source_target_pairs={{8,0},{16,8},{24,16},{28,24},{20,28},{12,20},{4,12},{0,4},{9,1},{1... | collective-permute-start | bytes 3538952 | tf_op jit(solution)/shard_map/ppermute | solution.py:51
  146.4 25.4 %collective-permute-start.28 = (bf16[128,1536]{1,0:T(8,128)(2,1)S(1)}, bf16[128,1536]{1,0:T(8,128)(2,1)S(1)}, u32[]{:S(2)}, u32[]{:S(2)}) collective-permute-start(bf16[128,1536]{1,0:T(8,128)(2,1)S(1)} %add_convert_fusion.19), channel_id=1, source_target_pairs={{0,2},{1,3},{2,0},{3,1},{4,6},{5,7},{6,4},{7,5},{8,10},{9,11},{10,... | collective-permute-start | bytes 1179656 | tf_op jit(solution)/shard_map/ppermute | solution.py:215
  148.0 27.5 %collective-permute-start.29 = (bf16[1,192,1536]{2,1,0:T(8,128)(2,1)}, bf16[1,192,1536]{2,1,0:T(8,128)(2,1)}, u32[]{:S(2)}, u32[]{:S(2)}) collective-permute-start(bf16[1,192,1536]{2,1,0:T(8,128)(2,1)} %collective-permute-done.23.refs_7_), channel_id=1, source_target_pairs={{0,8},{8,16},{16,24},{24,28},{28,20},{20,12},{12,4},{4,0},{1,9},{9... | collective-permute-start | bytes 1769480 | tf_op jit(solution)/shard_map/ppermute | solution.py:48
  148.6 26.8 %collective-permute-start.30 = (bf16[1,192,1536]{2,1,0:T(8,128)(2,1)}, bf16[1,192,1536]{2,1,0:T(8,128)(2,1)}, u32[]{:S(2)}, u32[]{:S(2)}) collective-permute-start(bf16[1,192,1536]{2,1,0:T(8,128)(2,1)} %collective-permute-done.24.refs_2_), channel_id=1, source_target_pairs={{8,0},{16,8},{24,16},{28,24},{20,28},{12,20},{4,12},{0,4},{9,1},{1... | collective-permute-start | bytes 1769480 | tf_op jit(solution)/shard_map/ppermute | solution.py:51
  172.6 16.1 %collective-permute-start.32 = (bf16[2,96,1536]{2,1,0:T(8,128)(2,1)}, bf16[2,96,1536]{2,1,0:T(8,128)(2,1)}, u32[]{:S(2)}, u32[]{:S(2)}) collective-permute-start(bf16[2,96,1536]{2,1,0:T(8,128)(2,1)} %slice.463), channel_id=1, source_target_pairs={{0,8},{8,16},{16,24},{24,28},{28,20},{20,12},{12,4},{4,0},{1,9},{9... | collective-permute-start | bytes 1769480 | tf_op jit(solution)/shard_map/ppermute | solution.py:48
  173.3 15.8 %collective-permute-start.33 = (bf16[2,96,1536]{2,1,0:T(8,128)(2,1)}, bf16[2,96,1536]{2,1,0:T(8,128)(2,1)}, u32[]{:S(2)}, u32[]{:S(2)}) collective-permute-start(bf16[2,96,1536]{2,1,0:T(8,128)(2,1)} %slice.464), channel_id=1, source_target_pairs={{8,0},{16,8},{24,16},{28,24},{20,28},{12,20},{4,12},{0,4},{9,1},{1... | collective-permute-start | bytes 1769480 | tf_op jit(solution)/shard_map/ppermute | solution.py:51
  189.1 21.4 %collective-permute-start.36 = (bf16[1,192,1536]{2,1,0:T(8,128)(2,1)S(1)}, bf16[1,192,1536]{2,1,0:T(8,128)(2,1)}, u32[]{:S(2)}, u32[]{:S(2)}) collective-permute-start(bf16[1,192,1536]{2,1,0:T(8,128)(2,1)S(1)} %copy-done.37), channel_id=1, source_target_pairs={{0,8},{8,16},{16,24},{24,28},{28,20},{20,12},{12,4},{4,0},{1,9},{9... | collective-permute-start | bytes 1769480 | tf_op jit(solution)/shard_map/ppermute | solution.py:48
  189.8 20.7 %collective-permute-start.37 = (bf16[1,192,1536]{2,1,0:T(8,128)(2,1)S(1)}, bf16[1,192,1536]{2,1,0:T(8,128)(2,1)}, u32[]{:S(2)}, u32[]{:S(2)}) collective-permute-start(bf16[1,192,1536]{2,1,0:T(8,128)(2,1)S(1)} %copy-done.37), channel_id=1, source_target_pairs={{8,0},{16,8},{24,16},{28,24},{20,28},{12,20},{4,12},{0,4},{9,1},{1... | collective-permute-start | bytes 1769480 | tf_op jit(solution)/shard_map/ppermute | solution.py:51
  192.8 17.3 %collective-permute-start.34 = (bf16[1,96,1536]{2,1,0:T(8,128)(2,1)S(1)}, bf16[1,96,1536]{2,1,0:T(8,128)(2,1)S(1)}, u32[]{:S(2)}, u32[]{:S(2)}) collective-permute-start(bf16[1,96,1536]{2,1,0:T(8,128)(2,1)S(1)} %slice.465), channel_id=1, source_target_pairs={{0,8},{8,16},{16,24},{24,28},{28,20},{20,12},{12,4},{4,0},{1,9},{9... | collective-permute-start | bytes 884744 | tf_op jit(solution)/shard_map/ppermute | solution.py:48
  193.5 17.0 %collective-permute-start.35 = (bf16[1,96,1536]{2,1,0:T(8,128)(2,1)S(1)}, bf16[1,96,1536]{2,1,0:T(8,128)(2,1)S(1)}, u32[]{:S(2)}, u32[]{:S(2)}) collective-permute-start(bf16[1,96,1536]{2,1,0:T(8,128)(2,1)S(1)} %slice.466), channel_id=1, source_target_pairs={{8,0},{16,8},{24,16},{28,24},{20,28},{12,20},{4,12},{0,4},{9,1},{1... | collective-permute-start | bytes 884744 | tf_op jit(solution)/shard_map/ppermute | solution.py:51
  211.8 16.2 %collective-permute-start.39 = (bf16[1,192,1536]{2,1,0:T(8,128)(2,1)S(1)}, bf16[1,192,1536]{2,1,0:T(8,128)(2,1)S(1)}, u32[]{:S(2)}, u32[]{:S(2)}) collective-permute-start(bf16[1,192,1536]{2,1,0:T(8,128)(2,1)S(1)} %copy-done.38), channel_id=1, source_target_pairs={{0,8},{8,16},{16,24},{24,28},{28,20},{20,12},{12,4},{4,0},{1,9},{9... | collective-permute-start | bytes 1769480 | tf_op jit(solution)/shard_map/ppermute | solution.py:48
  212.4 16.2 %collective-permute-start.40 = (bf16[1,192,1536]{2,1,0:T(8,128)(2,1)S(1)}, bf16[1,192,1536]{2,1,0:T(8,128)(2,1)S(1)}, u32[]{:S(2)}, u32[]{:S(2)}) collective-permute-start(bf16[1,192,1536]{2,1,0:T(8,128)(2,1)S(1)} %copy-done.38), channel_id=1, source_target_pairs={{8,0},{16,8},{24,16},{28,24},{20,28},{12,20},{4,12},{0,4},{9,1},{1... | collective-permute-start | bytes 1769480 | tf_op jit(solution)/shard_map/ppermute | solution.py:51
  217.1 23.1 %collective-permute-start.42 = (bf16[1,192,1536]{2,1,0:T(8,128)(2,1)}, bf16[1,192,1536]{2,1,0:T(8,128)(2,1)S(1)}, u32[]{:S(2)}, u32[]{:S(2)}) collective-permute-start(bf16[1,192,1536]{2,1,0:T(8,128)(2,1)} %collective-permute-done.36.refs_8_), channel_id=1, source_target_pairs={{0,8},{8,16},{16,24},{24,28},{28,20},{20,12},{12,4},{4,0},{1,9},{9... | collective-permute-start | bytes 1769480 | tf_op jit(solution)/shard_map/ppermute | solution.py:48
  217.7 22.8 %collective-permute-start.43 = (bf16[1,192,1536]{2,1,0:T(8,128)(2,1)}, bf16[1,192,1536]{2,1,0:T(8,128)(2,1)S(1)}, u32[]{:S(2)}, u32[]{:S(2)}) collective-permute-start(bf16[1,192,1536]{2,1,0:T(8,128)(2,1)} %collective-permute-done.37.refs_1_), channel_id=1, source_target_pairs={{8,0},{16,8},{24,16},{28,24},{20,28},{12,20},{4,12},{0,4},{9,1},{1... | collective-permute-start | bytes 1769480 | tf_op jit(solution)/shard_map/ppermute | solution.py:51
  240.7 15.7 %collective-permute-start.46 = (bf16[1,192,1536]{2,1,0:T(8,128)(2,1)S(1)}, bf16[1,192,1536]{2,1,0:T(8,128)(2,1)S(1)}, u32[]{:S(2)}, u32[]{:S(2)}) collective-permute-start(bf16[1,192,1536]{2,1,0:T(8,128)(2,1)S(1)} %collective-permute-done.39.refs_17_.refs_8_), channel_id=1, source_target_pairs={{0,8},{8,16},{16,24},{24,28},{28,20},{20,12},{12,4},{4,0},{1,9},{9... | collective-permute-start | bytes 1769480 | tf_op jit(solution)/shard_map/ppermute | solution.py:48
  241.3 15.8 %collective-permute-start.47 = (bf16[1,192,1536]{2,1,0:T(8,128)(2,1)S(1)}, bf16[1,192,1536]{2,1,0:T(8,128)(2,1)S(1)}, u32[]{:S(2)}, u32[]{:S(2)}) collective-permute-start(bf16[1,192,1536]{2,1,0:T(8,128)(2,1)S(1)} %collective-permute-done.40.refs_10_.refs_1_), channel_id=1, source_target_pairs={{8,0},{16,8},{24,16},{28,24},{20,28},{12,20},{4,12},{0,4},{9,1},{1... | collective-permute-start | bytes 1769480 | tf_op jit(solution)/shard_map/ppermute | solution.py:51
  257.2 16.2 %collective-permute-start.49 = (bf16[1,192,1536]{2,1,0:T(8,128)(2,1)S(1)}, bf16[1,192,1536]{2,1,0:T(8,128)(2,1)S(1)}, u32[]{:S(2)}, u32[]{:S(2)}) collective-permute-start(bf16[1,192,1536]{2,1,0:T(8,128)(2,1)S(1)} %collective-permute-done.42.refs_7_), channel_id=1, source_target_pairs={{0,8},{8,16},{16,24},{24,28},{28,20},{20,12},{12,4},{4,0},{1,9},{9... | collective-permute-start | bytes 1769480 | tf_op jit(solution)/shard_map/ppermute | solution.py:48
  258.8 16.2 %collective-permute-start.50 = (bf16[1,192,1536]{2,1,0:T(8,128)(2,1)S(1)}, bf16[1,192,1536]{2,1,0:T(8,128)(2,1)S(1)}, u32[]{:S(2)}, u32[]{:S(2)}) collective-permute-start(bf16[1,192,1536]{2,1,0:T(8,128)(2,1)S(1)} %collective-permute-done.43.refs_2_), channel_id=1, source_target_pairs={{8,0},{16,8},{24,16},{28,24},{20,28},{12,20},{4,12},{0,4},{9,1},{1... | collective-permute-start | bytes 1769480 | tf_op jit(solution)/shard_map/ppermute | solution.py:51
  259.8 17.3 %collective-permute-start.51 = (bf16[128,1536]{1,0:T(8,128)(2,1)S(1)}, bf16[128,1536]{1,0:T(8,128)(2,1)S(1)}, u32[]{:S(2)}, u32[]{:S(2)}) collective-permute-start(bf16[128,1536]{1,0:T(8,128)(2,1)S(1)} %dynamic-slice_convert_fusion.5), channel_id=1, source_target_pairs={{0,2},{1,3},{2,0},{3,1},{4,6},{5,7},{6,4},{7,5},{8,10},{9,11},{10,... | collective-permute-start | bytes 1179656 | tf_op jit(solution)/shard_map/ppermute | solution.py:215
  261.3 24.7 %collective-permute-start.52 = (bf16[1,192,1536]{2,1,0:T(8,128)(2,1)S(1)}, bf16[1,192,1536]{2,1,0:T(8,128)(2,1)S(1)}, u32[]{:S(2)}, u32[]{:S(2)}) collective-permute-start(bf16[1,192,1536]{2,1,0:T(8,128)(2,1)S(1)} %collective-permute-done.46.refs_16_.refs_7_), channel_id=1, source_target_pairs={{0,8},{8,16},{16,24},{24,28},{28,20},{20,12},{12,4},{4,0},{1,9},{9... | collective-permute-start | bytes 1769480 | tf_op jit(solution)/shard_map/ppermute | solution.py:48
  262.9 24.7 %collective-permute-start.53 = (bf16[1,192,1536]{2,1,0:T(8,128)(2,1)S(1)}, bf16[1,192,1536]{2,1,0:T(8,128)(2,1)S(1)}, u32[]{:S(2)}, u32[]{:S(2)}) collective-permute-start(bf16[1,192,1536]{2,1,0:T(8,128)(2,1)S(1)} %collective-permute-done.47.refs_11_.refs_2_), channel_id=1, source_target_pairs={{8,0},{16,8},{24,16},{28,24},{20,28},{12,20},{4,12},{0,4},{9,1},{1... | collective-permute-start | bytes 1769480 | tf_op jit(solution)/shard_map/ppermute | solution.py:51
  275.0 16.9 %collective-permute-start.54 = (bf16[1,96,1536]{2,1,0:T(8,128)(2,1)S(1)}, bf16[1,96,1536]{2,1,0:T(8,128)(2,1)S(1)}, u32[]{:S(2)}, u32[]{:S(2)}) collective-permute-start(bf16[1,96,1536]{2,1,0:T(8,128)(2,1)S(1)} %slice.474), channel_id=1, source_target_pairs={{0,8},{8,16},{16,24},{24,28},{28,20},{20,12},{12,4},{4,0},{1,9},{9... | collective-permute-start | bytes 884744 | tf_op jit(solution)/shard_map/ppermute | solution.py:48
  276.6 16.6 %collective-permute-start.55 = (bf16[1,96,1536]{2,1,0:T(8,128)(2,1)S(1)}, bf16[1,96,1536]{2,1,0:T(8,128)(2,1)}, u32[]{:S(2)}, u32[]{:S(2)}) collective-permute-start(bf16[1,96,1536]{2,1,0:T(8,128)(2,1)S(1)} %slice.475), channel_id=1, source_target_pairs={{8,0},{16,8},{24,16},{28,24},{20,28},{12,20},{4,12},{0,4},{9,1},{1... | collective-permute-start | bytes 884744 | tf_op jit(solution)/shard_map/ppermute | solution.py:51
  277.8 15.5 %collective-permute-start.56 = (bf16[128,1536]{1,0:T(8,128)(2,1)S(1)}, bf16[128,1536]{1,0:T(8,128)(2,1)S(1)}, u32[]{:S(2)}, u32[]{:S(2)}) collective-permute-start(bf16[128,1536]{1,0:T(8,128)(2,1)S(1)} %add_convert_fusion.16), channel_id=1, source_target_pairs={{0,2},{1,3},{2,0},{3,1},{4,6},{5,7},{6,4},{7,5},{8,10},{9,11},{10,... | collective-permute-start | bytes 1179656 | tf_op jit(solution)/shard_map/ppermute | solution.py:215
  298.0 15.4 %collective-permute-start.58 = (bf16[1,96,1536]{2,1,0:T(8,128)(2,1)}, bf16[1,96,1536]{2,1,0:T(8,128)(2,1)}, u32[]{:S(2)}, u32[]{:S(2)}) collective-permute-start(bf16[1,96,1536]{2,1,0:T(8,128)(2,1)} %slice.478), channel_id=1, source_target_pairs={{0,8},{8,16},{16,24},{24,28},{28,20},{20,12},{12,4},{4,0},{1,9},{9... | collective-permute-start | bytes 884744 | tf_op jit(solution)/shard_map/ppermute | solution.py:48
  353.0 26.6 %collective-permute-start.66 = (bf16[2,192,1536]{2,1,0:T(8,128)(2,1)S(1)}, bf16[2,192,1536]{2,1,0:T(8,128)(2,1)S(1)}, u32[]{:S(2)}, u32[]{:S(2)}) collective-permute-start(bf16[2,192,1536]{2,1,0:T(8,128)(2,1)S(1)} %fusion.34), channel_id=1, source_target_pairs={{0,8},{8,16},{16,24},{24,28},{28,20},{20,12},{12,4},{4,0},{1,9},{9... | collective-permute-start | bytes 3538952 | tf_op jit(solution)/shard_map/ppermute | solution.py:48
  354.5 26.4 %collective-permute-start.67 = (bf16[2,192,1536]{2,1,0:T(8,128)(2,1)S(1)}, bf16[2,192,1536]{2,1,0:T(8,128)(2,1)S(1)}, u32[]{:S(2)}, u32[]{:S(2)}) collective-permute-start(bf16[2,192,1536]{2,1,0:T(8,128)(2,1)S(1)} %pad_maximum_fusion.1), channel_id=1, source_target_pairs={{8,0},{16,8},{24,16},{28,24},{20,28},{12,20},{4,12},{0,4},{9,1},{1... | collective-permute-start | bytes 3538952 | tf_op jit(solution)/shard_map/ppermute | solution.py:51
  385.8 28.8 %collective-permute-start.70 = (bf16[2,192,1536]{2,1,0:T(8,128)(2,1)S(1)}, bf16[2,192,1536]{2,1,0:T(8,128)(2,1)S(1)}, u32[]{:S(2)}, u32[]{:S(2)}) collective-permute-start(bf16[2,192,1536]{2,1,0:T(8,128)(2,1)S(1)} %add_convert_fusion.7), channel_id=1, source_target_pairs={{0,8},{8,16},{16,24},{24,28},{28,20},{20,12},{12,4},{4,0},{1,9},{9... | collective-permute-start | bytes 3538952 | tf_op jit(solution)/shard_map/ppermute | solution.py:48
  386.8 28.8 %collective-permute-start.71 = (bf16[2,192,1536]{2,1,0:T(8,128)(2,1)S(1)}, bf16[2,192,1536]{2,1,0:T(8,128)(2,1)S(1)}, u32[]{:S(2)}, u32[]{:S(2)}) collective-permute-start(bf16[2,192,1536]{2,1,0:T(8,128)(2,1)S(1)} %add_convert_fusion.6), channel_id=1, source_target_pairs={{8,0},{16,8},{24,16},{28,24},{20,28},{12,20},{4,12},{0,4},{9,1},{1... | collective-permute-start | bytes 3538952 | tf_op jit(solution)/shard_map/ppermute | solution.py:51
  387.9 33.8 %collective-permute-start.73 = (bf16[1,96,1536]{2,1,0:T(8,128)(2,1)S(1)}, bf16[1,96,1536]{2,1,0:T(8,128)(2,1)S(1)}, u32[]{:S(2)}, u32[]{:S(2)}) collective-permute-start(bf16[1,96,1536]{2,1,0:T(8,128)(2,1)S(1)} %get-tuple-element.414), channel_id=1, source_target_pairs={{0,8},{8,16},{16,24},{24,28},{28,20},{20,12},{12,4},{4,0},{1,9},{9... | collective-permute-start | bytes 884744 | tf_op jit(solution)/shard_map/ppermute | solution.py:48
  388.8 33.1 %collective-permute-start.74 = (bf16[1,96,1536]{2,1,0:T(8,128)(2,1)S(1)}, bf16[1,96,1536]{2,1,0:T(8,128)(2,1)S(1)}, u32[]{:S(2)}, u32[]{:S(2)}) collective-permute-start(bf16[1,96,1536]{2,1,0:T(8,128)(2,1)S(1)} %get-tuple-element.415), channel_id=1, source_target_pairs={{8,0},{16,8},{24,16},{28,24},{20,28},{12,20},{4,12},{0,4},{9,1},{1... | collective-permute-start | bytes 884744 | tf_op jit(solution)/shard_map/ppermute | solution.py:51
  402.3 19.2 %collective-permute-start.72 = (bf16[128,1536]{1,0:T(8,128)(2,1)S(1)}, bf16[128,1536]{1,0:T(8,128)(2,1)S(1)}, u32[]{:S(2)}, u32[]{:S(2)}) collective-permute-start(bf16[128,1536]{1,0:T(8,128)(2,1)S(1)} %get-tuple-element.413), channel_id=1, source_target_pairs={{0,2},{1,3},{2,0},{3,1},{4,6},{5,7},{6,4},{7,5},{8,10},{9,11},{10,... | collective-permute-start | bytes 1179656 | tf_op jit(solution)/shard_map/ppermute | solution.py:215
  418.2 36.2 %collective-permute-start.76 = (bf16[2,192,1536]{2,1,0:T(8,128)(2,1)}, bf16[2,192,1536]{2,1,0:T(8,128)(2,1)}, u32[]{:S(2)}, u32[]{:S(2)}) collective-permute-start(bf16[2,192,1536]{2,1,0:T(8,128)(2,1)} %add_convert_fusion.5), channel_id=1, source_target_pairs={{0,8},{8,16},{16,24},{24,28},{28,20},{20,12},{12,4},{4,0},{1,9},{9... | collective-permute-start | bytes 3538952 | tf_op jit(solution)/shard_map/ppermute | solution.py:48
  419.1 35.3 %collective-permute-start.77 = (bf16[2,192,1536]{2,1,0:T(8,128)(2,1)}, bf16[2,192,1536]{2,1,0:T(8,128)(2,1)}, u32[]{:S(2)}, u32[]{:S(2)}) collective-permute-start(bf16[2,192,1536]{2,1,0:T(8,128)(2,1)} %add_convert_fusion.4), channel_id=1, source_target_pairs={{8,0},{16,8},{24,16},{28,24},{20,28},{12,20},{4,12},{0,4},{9,1},{1... | collective-permute-start | bytes 3538952 | tf_op jit(solution)/shard_map/ppermute | solution.py:51
  423.8 36.8 %collective-permute-start.79 = (bf16[1,192,1536]{2,1,0:T(8,128)(2,1)}, bf16[1,192,1536]{2,1,0:T(8,128)(2,1)}, u32[]{:S(2)}, u32[]{:S(2)}) collective-permute-start(bf16[1,192,1536]{2,1,0:T(8,128)(2,1)} %pad_maximum_fusion.9), channel_id=1, source_target_pairs={{0,8},{8,16},{16,24},{24,28},{28,20},{20,12},{12,4},{4,0},{1,9},{9... | collective-permute-start | bytes 1769480 | tf_op jit(solution)/shard_map/ppermute | solution.py:48
  424.7 35.9 %collective-permute-start.80 = (bf16[1,192,1536]{2,1,0:T(8,128)(2,1)}, bf16[1,192,1536]{2,1,0:T(8,128)(2,1)}, u32[]{:S(2)}, u32[]{:S(2)}) collective-permute-start(bf16[1,192,1536]{2,1,0:T(8,128)(2,1)} %pad_maximum_fusion.10), channel_id=1, source_target_pairs={{8,0},{16,8},{24,16},{28,24},{20,28},{12,20},{4,12},{0,4},{9,1},{1... | collective-permute-start | bytes 1769480 | tf_op jit(solution)/shard_map/ppermute | solution.py:51
  455.9 17.9 %collective-permute-start.82 = (bf16[2,96,1536]{2,1,0:T(8,128)(2,1)S(1)}, bf16[2,96,1536]{2,1,0:T(8,128)(2,1)S(1)}, u32[]{:S(2)}, u32[]{:S(2)}) collective-permute-start(bf16[2,96,1536]{2,1,0:T(8,128)(2,1)S(1)} %pad_maximum_fusion.11), channel_id=1, source_target_pairs={{0,8},{8,16},{16,24},{24,28},{28,20},{20,12},{12,4},{4,0},{1,9},{9... | collective-permute-start | bytes 1769480 | tf_op jit(solution)/shard_map/ppermute | solution.py:48
  456.9 17.0 %collective-permute-start.83 = (bf16[2,96,1536]{2,1,0:T(8,128)(2,1)S(1)}, bf16[2,96,1536]{2,1,0:T(8,128)(2,1)S(1)}, u32[]{:S(2)}, u32[]{:S(2)}) collective-permute-start(bf16[2,96,1536]{2,1,0:T(8,128)(2,1)S(1)} %pad_maximum_fusion.12), channel_id=1, source_target_pairs={{8,0},{16,8},{24,16},{28,24},{20,28},{12,20},{4,12},{0,4},{9,1},{1... | collective-permute-start | bytes 1769480 | tf_op jit(solution)/shard_map/ppermute | solution.py:51
  485.7 29.0 %collective-permute-start.86 = (bf16[1,192,1536]{2,1,0:T(8,128)(2,1)}, bf16[1,192,1536]{2,1,0:T(8,128)(2,1)}, u32[]{:S(2)}, u32[]{:S(2)}) collective-permute-start(bf16[1,192,1536]{2,1,0:T(8,128)(2,1)} %get-tuple-element.446), channel_id=1, source_target_pairs={{0,8},{8,16},{16,24},{24,28},{28,20},{20,12},{12,4},{4,0},{1,9},{9... | collective-permute-start | bytes 1769480 | tf_op jit(solution)/shard_map/ppermute | solution.py:48
  486.6 28.2 %collective-permute-start.87 = (bf16[1,192,1536]{2,1,0:T(8,128)(2,1)}, bf16[1,192,1536]{2,1,0:T(8,128)(2,1)}, u32[]{:S(2)}, u32[]{:S(2)}) collective-permute-start(bf16[1,192,1536]{2,1,0:T(8,128)(2,1)} %get-tuple-element.447), channel_id=1, source_target_pairs={{8,0},{16,8},{24,16},{28,24},{20,28},{12,20},{4,12},{0,4},{9,1},{1... | collective-permute-start | bytes 1769480 | tf_op jit(solution)/shard_map/ppermute | solution.py:51
  492.3 34.6 %collective-permute-start.88 = (bf16[2,192,1536]{2,1,0:T(8,128)(2,1)}, bf16[2,192,1536]{2,1,0:T(8,128)(2,1)S(1)}, u32[]{:S(2)}, u32[]{:S(2)}) collective-permute-start(bf16[2,192,1536]{2,1,0:T(8,128)(2,1)} %fusion.36), channel_id=1, source_target_pairs={{0,8},{8,16},{16,24},{24,28},{28,20},{20,12},{12,4},{4,0},{1,9},{9... | collective-permute-start | bytes 3538952 | tf_op jit(solution)/shard_map/ppermute | solution.py:48
  493.2 34.3 %collective-permute-start.89 = (bf16[2,192,1536]{2,1,0:T(8,128)(2,1)}, bf16[2,192,1536]{2,1,0:T(8,128)(2,1)S(1)}, u32[]{:S(2)}, u32[]{:S(2)}) collective-permute-start(bf16[2,192,1536]{2,1,0:T(8,128)(2,1)} %pad_maximum_fusion.2), channel_id=1, source_target_pairs={{8,0},{16,8},{24,16},{28,24},{20,28},{12,20},{4,12},{0,4},{9,1},{1... | collective-permute-start | bytes 3538952 | tf_op jit(solution)/shard_map/ppermute | solution.py:51
  530.2 16.1 %collective-permute-start.91 = (bf16[1,192,1536]{2,1,0:T(8,128)(2,1)S(1)}, bf16[1,192,1536]{2,1,0:T(8,128)(2,1)S(1)}, u32[]{:S(2)}, u32[]{:S(2)}) collective-permute-start(bf16[1,192,1536]{2,1,0:T(8,128)(2,1)S(1)} %get-tuple-element.458), channel_id=1, source_target_pairs={{0,8},{8,16},{16,24},{24,28},{28,20},{20,12},{12,4},{4,0},{1,9},{9... | collective-permute-start | bytes 1769480 | tf_op jit(solution)/shard_map/ppermute | solution.py:48
  531.0 16.2 %collective-permute-start.92 = (bf16[1,192,1536]{2,1,0:T(8,128)(2,1)S(1)}, bf16[1,192,1536]{2,1,0:T(8,128)(2,1)S(1)}, u32[]{:S(2)}, u32[]{:S(2)}) collective-permute-start(bf16[1,192,1536]{2,1,0:T(8,128)(2,1)S(1)} %get-tuple-element.459), channel_id=1, source_target_pairs={{8,0},{16,8},{24,16},{28,24},{20,28},{12,20},{4,12},{0,4},{9,1},{1... | collective-permute-start | bytes 1769480 | tf_op jit(solution)/shard_map/ppermute | solution.py:51
  532.2 39.1 %collective-permute-start.96 = (bf16[2,192,1536]{2,1,0:T(8,128)(2,1)}, bf16[2,192,1536]{2,1,0:T(8,128)(2,1)}, u32[]{:S(2)}, u32[]{:S(2)}) collective-permute-start(bf16[2,192,1536]{2,1,0:T(8,128)(2,1)} %add_convert_fusion.3), channel_id=1, source_target_pairs={{0,8},{8,16},{16,24},{24,28},{28,20},{20,12},{12,4},{4,0},{1,9},{9... | collective-permute-start | bytes 3538952 | tf_op jit(solution)/shard_map/ppermute | solution.py:48
  533.0 38.8 %collective-permute-start.97 = (bf16[2,192,1536]{2,1,0:T(8,128)(2,1)}, bf16[2,192,1536]{2,1,0:T(8,128)(2,1)}, u32[]{:S(2)}, u32[]{:S(2)}) collective-permute-start(bf16[2,192,1536]{2,1,0:T(8,128)(2,1)} %add_convert_fusion.2), channel_id=1, source_target_pairs={{8,0},{16,8},{24,16},{28,24},{20,28},{12,20},{4,12},{0,4},{9,1},{1... | collective-permute-start | bytes 3538952 | tf_op jit(solution)/shard_map/ppermute | solution.py:51
  579.3 34.3 %collective-permute-start.102 = (bf16[2,192,1536]{2,1,0:T(8,128)(2,1)}, bf16[2,192,1536]{2,1,0:T(8,128)(2,1)}, u32[]{:S(2)}, u32[]{:S(2)}) collective-permute-start(bf16[2,192,1536]{2,1,0:T(8,128)(2,1)} %add_convert_fusion.1), channel_id=1, source_target_pairs={{0,8},{8,16},{16,24},{24,28},{28,20},{20,12},{12,4},{4,0},{1,9},{9... | collective-permute-start | bytes 3538952 | tf_op jit(solution)/shard_map/ppermute | solution.py:48
  580.0 33.5 %collective-permute-start.103 = (bf16[2,192,1536]{2,1,0:T(8,128)(2,1)}, bf16[2,192,1536]{2,1,0:T(8,128)(2,1)}, u32[]{:S(2)}, u32[]{:S(2)}) collective-permute-start(bf16[2,192,1536]{2,1,0:T(8,128)(2,1)} %add_convert_fusion), channel_id=1, source_target_pairs={{8,0},{16,8},{24,16},{28,24},{20,28},{12,20},{4,12},{0,4},{9,1},{1... | collective-permute-start | bytes 3538952 | tf_op jit(solution)/shard_map/ppermute | solution.py:51
  590.1 35.5 %collective-permute-start.105 = (bf16[1,208,1536]{2,1,0:T(8,128)(2,1)}, bf16[1,208,1536]{2,1,0:T(8,128)(2,1)}, u32[]{:S(2)}, u32[]{:S(2)}) collective-permute-start(bf16[1,208,1536]{2,1,0:T(8,128)(2,1)} %pad_maximum_fusion.3), channel_id=1, source_target_pairs={{0,8},{8,16},{16,24},{24,28},{28,20},{20,12},{12,4},{4,0},{1,9},{9... | collective-permute-start | bytes 1916936 | tf_op jit(solution)/shard_map/ppermute | solution.py:48
  590.8 34.8 %collective-permute-start.106 = (bf16[1,208,1536]{2,1,0:T(8,128)(2,1)}, bf16[1,208,1536]{2,1,0:T(8,128)(2,1)}, u32[]{:S(2)}, u32[]{:S(2)}) collective-permute-start(bf16[1,208,1536]{2,1,0:T(8,128)(2,1)} %pad_maximum_fusion.4), channel_id=1, source_target_pairs={{8,0},{16,8},{24,16},{28,24},{20,28},{12,20},{4,12},{0,4},{9,1},{1... | collective-permute-start | bytes 1916936 | tf_op jit(solution)/shard_map/ppermute | solution.py:51
  646.9 16.7 %collective-permute-start.113 = (bf16[256,1536]{1,0:T(8,128)(2,1)S(1)}, bf16[256,1536]{1,0:T(8,128)(2,1)}, u32[]{:S(2)}, u32[]{:S(2)}) collective-permute-start(bf16[256,1536]{1,0:T(8,128)(2,1)S(1)} %constant_dynamic-update-slice_fusion.2), channel_id=1, source_target_pairs={{0,1},{1,0},{2,3},{3,2},{4,5},{5,4},{6,7},{7,6},{8,9},{9,8},{10,11... | collective-permute-start | bytes 2359304 | tf_op jit(solution)/shard_map/ppermute | solution.py:215
  (166 other events, 1645.7 us)
